TPU v7x, 32 devices: a whole 2x2x4 slice. The times are simulated.
32 devices in a mesh: section: 2 (over y), dp: 8 (over z, x), tensor: 2 (over core).
Axes of the slice: x: 2, y: 2, z: 4, core: 2. Of those that a mesh axis runs over, the one named last changes fastest.
Arguments:
- fwd_input: bfloat16 [2, 256, 2048], P('section', 'dp'), may hold values from -40 to 40
- fresh_input: bfloat16 [256, 2048], P('dp'), may hold values from -40 to 40
- cotangent: bfloat16 [2, 256, 2048], P('section', 'dp'), may hold values from -40 to 40
- fresh_cotangent: bfloat16 [256, 2048], P('dp'), may hold values from -40 to 40
- stash: bfloat16 [2, 2, 256, 2048], P('section', None, 'dp'), may hold values from -40 to 40
- norm_gain: float32 [2, 2048], P('section'), may hold values from 0.25 to 1.75
- qk_gain: float32 [2, 2, 128], P('section'), may hold values from 0.25 to 1.75
- w_query: bfloat16 [2, 2048, 2048], P('section', 'dp', 'tensor'), may hold values from -0.125 to 0.125
- w_key: bfloat16 [2, 2048, 256], P('section', 'dp', 'tensor'), may hold values from -0.125 to 0.125
- w_value: bfloat16 [2, 2048, 256], P('section', 'dp', 'tensor'), may hold values from -0.125 to 0.125
- w_out: bfloat16 [2, 2048, 2048], P('section', 'dp', 'tensor'), may hold values from -0.125 to 0.125
Outputs:
- out_activations: bfloat16 [2, 2, 256, 2048], P('section', None, 'dp')
- grad_input: bfloat16 [2, 2, 256, 2048], P('section', None, 'dp')
- grad_query: float32 [2, 2048, 2048], P('section', 'dp', 'tensor')
- grad_key: float32 [2, 2048, 256], P('section', 'dp', 'tensor')
- grad_value: float32 [2, 2048, 256], P('section', 'dp', 'tensor')
- grad_out: float32 [2, 2048, 2048], P('section', 'dp', 'tensor')
- grad_norm_gain: float32 [2, 2048], P('section')
- grad_qk_gain: float32 [2, 2, 128], P('section')
All inputs are finite; a program needn't handle non-finite values.
Results may differ from a plain program's by a relative error of at most 0.02.
Values may be sent and summed in bfloat16 or wider, within the bound.
A program may use at most 64 MiB of HBM per device.

v0:
```python
import math

import jax
import jax.numpy as jnp
from jax import lax
from jax.sharding import PartitionSpec as P

HD = 128


EPSILON = 1e-06
THETA = 1000000.0


def swapped(block, axis, apart):
    count = lax.axis_size(axis)
    route = []
    for low in range(count):
        high = low | 1 << apart
        if high != low and high < count:
            route += [(low, high), (high, low)]
    return lax.ppermute(block, axis, route)


def passed_along(array, axis, by):
    count = lax.axis_size(axis)
    pairs = [(i, i + by) for i in range(count) if 0 <= i + by < count]
    return lax.ppermute(array, axis, pairs)


def rope_tables(length, width):
    half_width = width // 2
    freqs = jnp.exp(jnp.arange(half_width, dtype=jnp.float32) * (-2.0 * math.log(THETA) / width))
    angles = jnp.arange(length, dtype=jnp.float32)[:, None] * freqs[None, :]
    return (jnp.cos(angles), jnp.sin(angles))


def rotate(vectors, cos_tab, sin_tab):
    half_width = vectors.shape[-1] // 2
    first_half = vectors[..., :half_width]
    second_half = vectors[..., half_width:]
    cos_here = cos_tab[:, None, :]
    sin_here = sin_tab[:, None, :]
    return jnp.concatenate(
        [
            first_half * cos_here - second_half * sin_here,
            second_half * cos_here + first_half * sin_here,
        ],
        axis=-1,
    )


def head_norm(raw_heads):
    inverse = lax.rsqrt(jnp.mean(raw_heads * raw_heads, axis=-1, keepdims=True) + EPSILON)
    return (raw_heads * inverse, inverse)


def unit_back(grad_unit, unit_row_vectors, inverse):
    return inverse * (
        grad_unit
        - unit_row_vectors * jnp.mean(grad_unit * unit_row_vectors, axis=-1, keepdims=True)
    )


def input_norm(x_rows, norm_scale):
    x_float = x_rows.astype(jnp.float32)
    inverse = lax.rsqrt(jnp.mean(x_float * x_float, axis=-1, keepdims=True) + EPSILON)
    unit_row_vectors = x_float * inverse
    return (
        x_float,
        inverse,
        unit_row_vectors,
        (unit_row_vectors * norm_scale).astype(jnp.bfloat16),
    )


def attend_local(normed, w_q, w_k, w_v, qk_gains, cos_tab, sin_tab):
    row_count = normed.shape[0]
    head_count = w_q.shape[1] // HD
    kv_count = w_k.shape[1] // HD
    group_size = head_count // kv_count
    q_unit, q_inv = head_norm(
        jnp.dot(normed, w_q, preferred_element_type=jnp.float32).reshape(row_count, head_count, HD)
    )
    k_unit, k_inv = head_norm(
        jnp.dot(normed, w_k, preferred_element_type=jnp.float32).reshape(row_count, kv_count, HD)
    )
    queries = (
        rotate(q_unit * qk_gains[0], cos_tab, sin_tab)
        .astype(jnp.bfloat16)
        .reshape(row_count, kv_count, group_size, HD)
    )
    keys_b = rotate(k_unit * qk_gains[1], cos_tab, sin_tab).astype(jnp.bfloat16)
    values_b = (
        jnp.dot(normed, w_v, preferred_element_type=jnp.float32)
        .astype(jnp.bfloat16)
        .reshape(row_count, kv_count, HD)
    )
    scores = jnp.einsum("qkgd,tkd->kgqt", queries, keys_b, preferred_element_type=jnp.float32) * (
        1.0 / math.sqrt(HD)
    )
    causal = lax.broadcasted_iota(jnp.int32, (row_count, row_count), 0) >= lax.broadcasted_iota(
        jnp.int32, (row_count, row_count), 1
    )
    expd = jnp.where(causal, jnp.exp(scores), 0.0)
    softmax_f = expd / jnp.sum(expd, axis=-1, keepdims=True)
    softmax_b = softmax_f.astype(jnp.bfloat16)
    attended = jnp.einsum("kgqt,tkd->qkgd", softmax_b, values_b, preferred_element_type=jnp.float32)
    attended = attended.reshape(row_count, head_count * HD).astype(jnp.bfloat16)
    return (q_unit, q_inv, k_unit, k_inv, queries, keys_b, values_b, softmax_f, softmax_b, attended)


def forward_part(x_rows, norm_scale, weights, qk_gains, cos_tab, sin_tab):
    w_q, w_k, w_v, w_o = weights
    x_float, inverse, unit_row_vectors, normed = input_norm(x_rows, norm_scale)
    attended = attend_local(normed, w_q, w_k, w_v, qk_gains, cos_tab, sin_tab)[-1]
    out_part = lax.dot_general(
        attended, w_o, (((1,), (1,)), ((), ())), preferred_element_type=jnp.float32
    )
    return (x_float, out_part)


def backward_part(x_rows, cot_rows, norm_scale, weights, qk_gains, cos_tab, sin_tab):
    w_q, w_k, w_v, w_o = weights
    x_float, inverse, unit_row_vectors, normed = input_norm(x_rows, norm_scale)
    q_unit, q_inv, k_unit, k_inv, queries, keys_b, values_b, softmax_f, softmax_b, attended = (
        attend_local(normed, w_q, w_k, w_v, qk_gains, cos_tab, sin_tab)
    )
    row_count, kv_count, group_size = (queries.shape[0], queries.shape[1], queries.shape[2])
    d_attn = (
        jnp.dot(cot_rows, w_o, preferred_element_type=jnp.float32)
        .astype(jnp.bfloat16)
        .reshape(row_count, kv_count, group_size, HD)
    )
    d_probs = jnp.einsum("qkgd,tkd->kgqt", d_attn, values_b, preferred_element_type=jnp.float32)
    d_value = jnp.einsum("kgqt,qkgd->tkd", softmax_b, d_attn, preferred_element_type=jnp.float32)
    d_value = d_value.astype(jnp.bfloat16).reshape(row_count, kv_count * HD)
    d_scores = (
        softmax_f
        * (d_probs - jnp.sum(softmax_f * d_probs, axis=-1, keepdims=True))
        * (1.0 / math.sqrt(HD))
    )
    d_scores = d_scores.astype(jnp.bfloat16)
    d_query = jnp.einsum(
        "kgqt,tkd->qkgd", d_scores, keys_b, preferred_element_type=jnp.float32
    ).reshape(row_count, kv_count * group_size, HD)
    d_key = jnp.einsum("kgqt,qkgd->tkd", d_scores, queries, preferred_element_type=jnp.float32)
    d_query = rotate(d_query, cos_tab, -sin_tab)
    d_key = rotate(d_key, cos_tab, -sin_tab)
    q_term = jnp.sum(d_query * q_unit, axis=(0, 1))
    k_term = jnp.sum(d_key * k_unit, axis=(0, 1))
    q_grad = (
        unit_back(d_query * qk_gains[0], q_unit, q_inv).astype(jnp.bfloat16).reshape(row_count, -1)
    )
    k_grad = (
        unit_back(d_key * qk_gains[1], k_unit, k_inv).astype(jnp.bfloat16).reshape(row_count, -1)
    )
    contract = (((1,), (1,)), ((), ()))
    normed_part = lax.dot_general(q_grad, w_q, contract, preferred_element_type=jnp.float32)
    normed_part = normed_part + lax.dot_general(
        k_grad, w_k, contract, preferred_element_type=jnp.float32
    )
    normed_part = normed_part + lax.dot_general(
        d_value, w_v, contract, preferred_element_type=jnp.float32
    )
    columns = jnp.concatenate([q_grad, k_grad, d_value], axis=1)
    return (normed_part, unit_row_vectors, inverse, normed, columns, attended, q_term, k_term)


def tensor_sums(out_part, normed_part):
    return (
        lax.psum(out_part.astype(jnp.bfloat16), "tensor").astype(jnp.float32),
        lax.psum(normed_part.astype(jnp.bfloat16), "tensor").astype(jnp.float32),
    )


def run_slot(x_forward, x_backward, cot_rows, norm_scale, weights, qk_gains, cos_tab, sin_tab):
    x_float, out_part = forward_part(x_forward, norm_scale, weights, qk_gains, cos_tab, sin_tab)
    normed_part, unit_row_vectors, inverse, normed, columns, attended, q_term, k_term = (
        backward_part(x_backward, cot_rows, norm_scale, weights, qk_gains, cos_tab, sin_tab)
    )
    out_sum, d_normed = tensor_sums(out_part, normed_part)
    layer_out = (x_float + out_sum).astype(jnp.bfloat16)
    d_input = (
        cot_rows.astype(jnp.float32) + unit_back(d_normed * norm_scale, unit_row_vectors, inverse)
    ).astype(jnp.bfloat16)
    norm_term = jnp.sum(d_normed * unit_row_vectors, axis=0)
    return (layer_out, d_input, normed, columns, attended, norm_term, q_term, k_term)


def local(
    fwd_input,
    fresh_input,
    cotangent,
    fresh_cotangent,
    stash,
    norm_gain,
    qk_gain,
    w_query,
    w_key,
    w_value,
    w_out,
):
    full_q, full_k, full_v, full_o = (
        lax.all_gather(w_query, "dp", axis=1, tiled=True),
        lax.all_gather(w_key, "dp", axis=1, tiled=True),
        lax.all_gather(w_value, "dp", axis=1, tiled=True),
        lax.all_gather(w_out, "dp", axis=1, tiled=True),
    )
    weights = (full_q[0], full_k[0], full_v[0], full_o[0])
    norm_scale = norm_gain[0]
    qk_gains = qk_gain[0]
    row_count = fwd_input.shape[1]
    cos_tab, sin_tab = rope_tables(row_count, HD)
    section_position_index = lax.axis_index("section")
    section_total = lax.axis_size("section")
    bit_order = list(range(section_total.bit_length() - 1))
    reloaded = stash[0]
    for bit_index in bit_order:
        reloaded = swapped(reloaded, "section", bit_index)
    first_slot = run_slot(
        fwd_input[0], reloaded[0], cotangent[0], norm_scale, weights, qk_gains, cos_tab, sin_tab
    )
    arrived = passed_along(first_slot[0], "section", 1)
    second_input = jnp.where(section_position_index == 0, fresh_input, arrived)
    returned = passed_along(first_slot[1], "section", -1)
    second_cot = jnp.where(section_position_index == section_total - 1, fresh_cotangent, returned)
    second_slot = run_slot(
        second_input, reloaded[1], second_cot, norm_scale, weights, qk_gains, cos_tab, sin_tab
    )
    out_activations = jnp.stack([first_slot[0], second_slot[0]])[None]
    grad_input = jnp.stack([first_slot[1], second_slot[1]])[None]
    grad_scale = 1.0 / math.sqrt(2 * row_count * lax.axis_size("dp"))
    normed_rows = jnp.concatenate([first_slot[2], second_slot[2]], axis=0)
    column_rows = jnp.concatenate([first_slot[3], second_slot[3]], axis=0)
    cot_rows = jnp.concatenate([cotangent[0], second_cot], axis=0)
    attended_rows = jnp.concatenate([first_slot[4], second_slot[4]], axis=0)
    contract = (((0,), (0,)), ((), ()))
    left_term = lax.dot_general(
        normed_rows, column_rows, contract, preferred_element_type=jnp.float32
    )
    right_term = lax.dot_general(
        cot_rows, attended_rows, contract, preferred_element_type=jnp.float32
    )
    owned = lax.psum_scatter(
        (jnp.concatenate([left_term, right_term], axis=1) * grad_scale).astype(jnp.bfloat16),
        "dp",
        scatter_dimension=0,
        tiled=True,
    ).astype(jnp.float32)
    q_width = w_query.shape[2]
    k_width = w_key.shape[2]
    grad_query = owned[:, :q_width][None]
    grad_key = owned[:, q_width : q_width + k_width][None]
    grad_value = owned[:, q_width + k_width : q_width + 2 * k_width][None]
    grad_out = owned[:, q_width + 2 * k_width :][None]
    norm_term = first_slot[5] + second_slot[5]
    feature_count = norm_term.shape[0]
    half_width = feature_count // lax.axis_size("tensor")
    feature_owner = lax.broadcasted_iota(jnp.int32, (feature_count,), 0) // half_width
    own_half = jnp.where(feature_owner == lax.axis_index("tensor"), norm_term, 0.0)
    qk_term = jnp.stack([first_slot[6] + second_slot[6], first_slot[7] + second_slot[7]])
    norm_total, qk_total = lax.psum((own_half * grad_scale, qk_term * grad_scale), ("dp", "tensor"))
    return (
        out_activations,
        grad_input,
        grad_query,
        grad_key,
        grad_value,
        grad_out,
        norm_total[None],
        qk_total[None],
    )


def solution(mesh):
    return jax.shard_map(
        local,
        mesh=mesh,
        in_specs=(
            P("section", "dp", None),
            P("dp", None),
            P("section", "dp", None),
            P("dp", None),
            P("section", None, "dp", None),
            P("section", None),
            P("section", None, None),
            P("section", "dp", "tensor"),
            P("section", "dp", "tensor"),
            P("section", "dp", "tensor"),
            P("section", "dp", "tensor"),
        ),
        out_specs=(
            P("section", None, "dp", None),
            P("section", None, "dp", None),
            P("section", "dp", "tensor"),
            P("section", "dp", "tensor"),
            P("section", "dp", "tensor"),
            P("section", "dp", "tensor"),
            P("section", None),
            P("section", None, None),
        ),
        check_vma=False,
    )
```

profile of v0, /device:TPU:12, one launch (start us, length us, event | category | flops | bytes accessed | tf_op | source)
XLA Modules:
  0.0 434.0 jit_solution(6396879940775473951)
XLA Ops:
  7.2 0.7 all-gather.3.cloned.1.call-update
  7.9 0.7 all-gather.5.cloned.1.call-update
  8.7 0.6 collective-permute-start.1
  9.3 1.0 fusion.91
  10.3 30.4 %all_gather.13 = bf16[1,2048,128]{2,1,0:T(8,128)(2,1)S(1)} all-gather(bf16[1,256,128]{2,1,0:T(8,128)(2,1)} %param.19), channel_id=1, replica_groups=mesh['section'=2,'dp'=8,'tensor'=2] {'dp'}, dimensions={1}, use_global_device_ids=true | all-gather | bytes 589824 | tf_op jit(solution)/shard_map/all_gather | solution.py:206
  40.8 1.3 multiply_reduce_fusion.17
  42.1 0.8 slice_bitcast_fusion.5
  42.9 33.1 %all_gather.12 = bf16[1,2048,128]{2,1,0:T(8,128)(2,1)S(1)} all-gather(bf16[1,256,128]{2,1,0:T(8,128)(2,1)} %param.20), channel_id=1, replica_groups=mesh['section'=2,'dp'=8,'tensor'=2] {'dp'}, dimensions={1}, use_global_device_ids=true | all-gather | bytes 589824 | tf_op jit(solution)/shard_map/all_gather | solution.py:207
  76.2 1.0 fusion.47
  77.2 1.1 multiply_reduce_fusion.15
  78.5 16.3 %all-gather.3.cloned.1.call-done = bf16[1,2048,1024]{2,1,0:T(8,128)(2,1)} async-done(((bf16[1,256,1024]{2,1,0:T(8,128)(2,1)}), bf16[1,2048,1024]{2,1,0:T(8,128)(2,1)}) %all-gather.3.cloned.1.call-update) | async-done | bytes 4194320 | tf_op jit(solution)/shard_map/all_gather | solution.py:205
  94.8 6.5 %copy.34 = bf16[1024,2048]{1,0:T(8,128)(2,1)} copy(bf16[1024,2048]{0,1:T(8,128)(2,1)} %bitcast.461) | data formatting | bytes 8388608 | tf_op jit(solution)/shard_map/dot_general | solution.py:83
  101.3 3.8 multiply_reduce_fusion.7
  105.1 1.5 multiply_reduce_fusion.9
  107.2 62.7 %all-gather.5.cloned.1.call-done = bf16[1,2048,1024]{2,1,0:T(8,128)(2,1)} async-done(((bf16[1,256,1024]{2,1,0:T(8,128)(2,1)}), bf16[1,2048,1024]{2,1,0:T(8,128)(2,1)}) %all-gather.5.cloned.1.call-update) | async-done | bytes 4194320 | tf_op jit(solution)/shard_map/all_gather | solution.py:208
  169.9 3.0 fusion.29
  175.6 3.8 fusion.9
  179.7 1.0 fusion.13
  180.7 2.0 fusion.15
  183.2 17.2 %all-reduce.8.cloned.1.call-done = (bf16[32,2048]{1,0:T(8,128)(2,1)}, bf16[32,2048]{1,0:T(8,128)(2,1)}) async-done(((bf16[32,2048]{1,0:T(8,128)(2,1)}, bf16[32,2048]{1,0:T(8,128)(2,1)}), (bf16[32,2048]{1,0:T(8,128)(2,1)}, bf16[32,2048]{1,0:T(8,128)(2,1)})) %all-reduce.8.cloned.1.call-update) | async-done | bytes 262160 | tf_op jit(solution)/shard_map/psum | solution.py:172
  200.3 1.1 fusion.92
  201.4 1.4 fusion.97
  202.8 1.1 fusion.96
  203.9 2.5 collective-permute-start.2
  206.4 1.5 collective-permute-start
  208.2 3.6 multiply_reduce_fusion.4
  212.2 1.5 collective-permute-done
  213.9 1.5 multiply_reduce_fusion.8
  216.6 0.8 fusion.32
  220.3 3.9 fusion.11
  224.5 1.0 fusion.14
  225.4 2.0 fusion.18
  227.5 4.5 %fusion.115 = f32[2048,1024]{0,1:T(8,128)} fusion(bf16[32,2048]{1,0:T(8,128)(2,1)S(1)} %broadcast_select_fusion, bf16[32,2048]{1,0:T(8,128)(2,1)S(1)} %bitcast.478, bf16[32,1024]{1,0:T(8,128)(2,1)S(1)} %bitcast.482, bf16[32,1024]{1,0:T(8,128)(2,1)S(1)} %bitcast.481), kind=kOutput, calls=%fused_computation.145 | convolution fusion | flops 269221888 | bytes 8781824 | tf_op jit(solution)/shard_map/dot_general | solution.py:242
  232.2 14.9 %all-reduce.6.cloned.1.call-done = (bf16[32,2048]{1,0:T(8,128)(2,1)}, bf16[32,2048]{1,0:T(8,128)(2,1)}) async-done(((bf16[32,2048]{1,0:T(8,128)(2,1)}, bf16[32,2048]{1,0:T(8,128)(2,1)}), (bf16[32,2048]{1,0:T(8,128)(2,1)}, bf16[32,2048]{1,0:T(8,128)(2,1)})) %all-reduce.6.cloned.1.call-update) | async-done | bytes 262160 | tf_op jit(solution)/shard_map/psum | solution.py:172
  247.1 1.2 fusion.103
  248.3 1.1 fusion.102
  249.3 1.6 fusion.111
  250.9 1.8 copy-done.5
  252.7 5.3 %fusion = bf16[2048,2304]{0,1:T(8,128)(2,1)} fusion(f32[2048,1024]{0,1:T(8,128)S(1)} %copy-done.5, f32[2048,1280]{0,1:T(8,128)S(1)} %fusion.111), kind=kLoop, calls=%fused_computation.1 | loop fusion | flops 14155776 | bytes 28311552 | tf_op jit(solution)/shard_map/convert_element_type | solution.py:246
  258.1 29.9 %all-reduce = (f32[1,2048]{1,0:T(1,128)}, f32[1,2,128]{2,1,0:T(2,128)}) all-reduce(f32[1,2048]{1,0:T(1,128)S(1)} %bitcast.491, f32[1,2,128]{2,1,0:T(2,128)S(1)} %fusion.192), channel_id=1, replica_groups=mesh['section'=2,'dp'=8,'tensor'=2] {'dp','tensor'}, use_global_device_ids=true, to_apply=%region_31.32 | all-reduce | flops 2304 | bytes 18432 | tf_op jit(solution)/shard_map/psum | solution.py:263
  288.0 0.7 maximum_bitcast_fusion
  288.7 0.7 maximum_bitcast_fusion.1
  289.4 132.3 %reduce-scatter.2.cloned.1.call-done = bf16[256,2304]{0,1:T(8,128)(2,1)} async-done(((bf16[2048,2304]{0,1:T(8,128)(2,1)}), bf16[256,2304]{0,1:T(8,128)(2,1)}) %reduce-scatter.2.cloned.1.call-update) | async-done | bytes 1179664 | tf_op jit(solution)/shard_map/reduce_scatter | solution.py:245
  421.7 1.4 convert_element_type.335
  423.3 1.3 copy.54
  424.7 0.8 copy.53
  425.4 0.8 copy.52
  426.2 1.3 copy.51
  (117 shorter events, 10.1 us)
Async XLA Ops:
  7.2 87.6 %all-gather.3.cloned.1.call-start = ((), (), s32[]{:S(2)}) async-start(), calls=%async_computation.1 | async-start | bytes 4718592 | tf_op jit(solution)/shard_map/all_gather | solution.py:205
  7.9 162.0 %all-gather.5.cloned.1.call-start = ((), (), s32[]{:S(2)}) async-start(), calls=%async_computation.2 | async-start | bytes 4718592 | tf_op jit(solution)/shard_map/all_gather | solution.py:208
  8.7 191.7 %all-reduce.8.cloned.1.call-start = ((), (), s32[]{:S(2)}) async-start(), calls=%async_computation.5 | async-start | bytes 524288 | tf_op jit(solution)/shard_map/psum | solution.py:172
  8.7 67.4 %collective-permute-start.1 = (bf16[2,32,2048]{2,1,0:T(8,128)(2,1)}, bf16[2,32,2048]{2,1,0:T(8,128)(2,1)S(1)}, u32[]{:S(2)}, u32[]{:S(2)}) collective-permute-start(bf16[2,32,2048]{2,1,0:T(8,128)(2,1)} %bitcast.492), channel_id=1, source_target_pairs={{0,16},{16,0},{1,17},{17,1},{2,18},{18,2},{3,19},{19,3},{4,20},{20... | collective-permute-start | bytes 786440 | tf_op jit(solution)/shard_map/ppermute | solution.py:22
  94.8 6.5 %copy-start.7 = (f32[1,2048]{1,0:T(1,128)S(1)}, f32[1,2048]{1,0:T(1,128)}, u32[]{:S(2)}) copy-start(f32[1,2048]{1,0:T(1,128)} %param.16) | copy-start | bytes 24580
  101.2 3.8 copy-start
  101.2 3.8 copy-start.6
  101.2 68.7 %copy-start.8 = (bf16[1,32,2048]{2,1,0:T(8,128)(2,1)S(1)}, bf16[1,32,2048]{2,1,0:T(8,128)(2,1)}, u32[]{:S(2)}) copy-start(bf16[1,32,2048]{2,1,0:T(8,128)(2,1)} %param.13) | copy-start | bytes 393220
  175.1 5.6 %copy-start.2 = (bf16[1,2048,1024]{2,1,0:T(8,128)(2,1)S(1)}, bf16[1,2048,1024]{2,1,0:T(8,128)(2,1)}, u32[]{:S(2)}) copy-start(bf16[1,2048,1024]{2,1,0:T(8,128)(2,1)} %all-gather.5.cloned.1.call-done) | copy-start | bytes 12582916
  182.7 31.0 %copy-start.9 = (bf16[32,2048]{1,0:T(8,128)(2,1)S(1)}, bf16[32,2048]{1,0:T(8,128)(2,1)}, u32[]{:S(2)}) copy-start(bf16[32,2048]{1,0:T(8,128)(2,1)} %param.12) | copy-start | bytes 393220
  182.7 64.4 %all-reduce.6.cloned.1.call-start = ((), (), s32[]{:S(2)}) async-start(), calls=%async_computation.4 | async-start | bytes 524288 | tf_op jit(solution)/shard_map/psum | solution.py:172
  200.3 13.5 %copy-start.1 = (bf16[1024,2048]{1,0:T(8,128)(2,1)S(1)}, bf16[1024,2048]{1,0:T(8,128)(2,1)}, u32[]{:S(2)}) copy-start(bf16[1024,2048]{1,0:T(8,128)(2,1)} %copy.34) | copy-start | bytes 12582916
  203.9 12.6 %collective-permute-start.2 = (bf16[32,2048]{1,0:T(8,128)(2,1)S(1)}, bf16[32,2048]{1,0:T(8,128)(2,1)S(1)}, u32[]{:S(2)}, u32[]{:S(2)}) collective-permute-start(bf16[32,2048]{1,0:T(8,128)(2,1)S(1)} %get-tuple-element.50), channel_id=1, source_target_pairs={{16,0},{17,1},{18,2},{19,3},{20,4},{21,5},{22,6},{23,7},{24,8},{25... | collective-permute-start | bytes 393224 | tf_op jit(solution)/shard_map/ppermute | solution.py:28
  206.4 7.3 %collective-permute-start = (bf16[32,2048]{1,0:T(8,128)(2,1)S(1)}, bf16[32,2048]{1,0:T(8,128)(2,1)S(1)}, u32[]{:S(2)}, u32[]{:S(2)}) collective-permute-start(bf16[32,2048]{1,0:T(8,128)(2,1)S(1)} %fusion.92), channel_id=1, source_target_pairs={{0,16},{1,17},{2,18},{3,19},{4,20},{5,21},{6,22},{7,23},{8,24},{9,... | collective-permute-start | bytes 393224 | tf_op jit(solution)/shard_map/ppermute | solution.py:28
  211.9 4.6 %copy-start.11 = (bf16[32,2048]{1,0:T(8,128)(2,1)S(1)}, bf16[32,2048]{1,0:T(8,128)(2,1)}, u32[]{:S(2)}) copy-start(bf16[32,2048]{1,0:T(8,128)(2,1)} %param.14) | copy-start | bytes 393220
  211.9 4.7 %copy-start.3 = (bf16[1,2048,1024]{2,1,0:T(8,128)(2,1)S(1)}, bf16[1,2048,1024]{2,1,0:T(8,128)(2,1)}, u32[]{:S(2)}) copy-start(bf16[1,2048,1024]{2,1,0:T(8,128)(2,1)} %all-gather.5.cloned.1.call-done) | copy-start | bytes 12582916
  219.7 5.7 %copy-start.4 = (bf16[1,2048,1024]{2,1,0:T(8,128)(2,1)S(1)}, bf16[1,2048,1024]{2,1,0:T(8,128)(2,1)}, u32[]{:S(2)}) copy-start(bf16[1,2048,1024]{2,1,0:T(8,128)(2,1)} %all-gather.5.cloned.1.call-done) | copy-start | bytes 12582916
  227.5 194.3 %reduce-scatter.2.cloned.1.call-start = ((), (), s32[]{:S(2)}) async-start(), calls=%async_computation.3 | async-start | bytes 10616832 | tf_op jit(solution)/shard_map/reduce_scatter | solution.py:245
  249.3 3.4 copy-start.5
  258.0 30.0 %copy-start.10 = (bf16[32,2048]{1,0:T(8,128)(2,1)S(1)}, bf16[32,2048]{1,0:T(8,128)(2,1)}, u32[]{:S(2)}) copy-start(bf16[32,2048]{1,0:T(8,128)(2,1)} %get-tuple-element.39) | copy-start | bytes 393220
Sparse Core Ops, SparseCore 0:
  10.1 84.5 all-gather.2
  96.9 72.9 all-gather.4
  182.8 17.4 all-reduce.7
  227.6 19.4 all-reduce.5
  258.1 163.5 reduce-scatter.1
where the time goes:
time: 438 us; the launch traced here: 434 us
  waiting for transfers between devices  246 us (56%)
  blocking collectives  93.5 us (21%)
  matrix products  42.9 us (10%)
  other arithmetic  18.4 us (4%)
  between operations  14.4 us (3%)
  local copies, waits for them, and re-layouts  13.8 us (3%)
  starting transfers between devices  4.7 us (1%)
    reduce_scatter x1, waiting for transfers between devices, local(): lax.psum_scatter((jnp.concatenate([left_term, right_term], axis=1) * grad...  132 us
    all_gather x1, waiting for transfers between devices, local(): lax.all_gather(w_out, 'dp', axis=1, tiled=True)  62.7 us
    all_gather x1, blocking collectives, local(): lax.all_gather(w_value, 'dp', axis=1, tiled=True)  33.1 us
    psum x2, waiting for transfers between devices, tensor_sums(): lax.psum(out_part.astype(jnp.bfloat16), 'tensor').astype(jnp.float32)  32.1 us
    all_gather x1, blocking collectives, local(): lax.all_gather(w_key, 'dp', axis=1, tiled=True)  30.4 us
    psum x1, blocking collectives, local(): lax.psum((own_half * grad_scale, qk_term * grad_scale), ('dp', 'tensor'))  29.9 us
    all_gather x1, waiting for transfers between devices, local(): lax.all_gather(w_query, 'dp', axis=1, tiled=True)  16.3 us
    dot_general x4, matrix products, attend_local(): jnp.dot(normed, w_q, preferred_element_type=jnp.float32)  10.3 us
  transfers between devices with their start and end apart: 8, of which 6 were waited for; matrix products, arithmetic and copies ran while one was open for 7% of the time, Pallas kernels for 0%

commit v1 on v0

--- a/solution.py
+++ b/solution.py
@@ -167,11 +167,20 @@
     return (normed_part, unit_row_vectors, inverse, normed, columns, attended, q_term, k_term)
 
 
+def tensor_sum(part):
+    count = lax.axis_size("tensor")
+    mine = part.astype(jnp.bfloat16)
+    total = mine.astype(jnp.float32)
+    for step in range(1, count):
+        route = [(i, i ^ step) for i in range(count)]
+        total = total + lax.ppermute(mine, "tensor", route).astype(jnp.float32)
+    return total
+
+
 def tensor_sums(out_part, normed_part):
-    return (
-        lax.psum(out_part.astype(jnp.bfloat16), "tensor").astype(jnp.float32),
-        lax.psum(normed_part.astype(jnp.bfloat16), "tensor").astype(jnp.float32),
-    )
+    both = tensor_sum(jnp.concatenate([out_part, normed_part], axis=0))
+    rows = out_part.shape[0]
+    return both[:rows], both[rows:]
 
 
 def run_slot(x_forward, x_backward, cot_rows, norm_scale, weights, qk_gains, cos_tab, sin_tab):
@@ -236,24 +245,27 @@
     cot_rows = jnp.concatenate([cotangent[0], second_cot], axis=0)
     attended_rows = jnp.concatenate([first_slot[4], second_slot[4]], axis=0)
     contract = (((0,), (0,)), ((), ()))
+    sliced = lax.all_to_all(
+        jnp.stack([normed_rows, cot_rows]), "dp", split_axis=2, concat_axis=1, tiled=True
+    )
+    gathered = lax.all_gather(
+        jnp.concatenate([column_rows, attended_rows], axis=1), "dp", axis=0, tiled=True
+    )
+    left_width = column_rows.shape[1]
     left_term = lax.dot_general(
-        normed_rows, column_rows, contract, preferred_element_type=jnp.float32
+        sliced[0], gathered[:, :left_width], contract, preferred_element_type=jnp.float32
     )
     right_term = lax.dot_general(
-        cot_rows, attended_rows, contract, preferred_element_type=jnp.float32
-    )
-    owned = lax.psum_scatter(
-        (jnp.concatenate([left_term, right_term], axis=1) * grad_scale).astype(jnp.bfloat16),
-        "dp",
-        scatter_dimension=0,
-        tiled=True,
-    ).astype(jnp.float32)
+        sliced[1], gathered[:, left_width:], contract, preferred_element_type=jnp.float32
+    )
+    left_term = left_term * grad_scale
+    right_term = right_term * grad_scale
     q_width = w_query.shape[2]
     k_width = w_key.shape[2]
-    grad_query = owned[:, :q_width][None]
-    grad_key = owned[:, q_width : q_width + k_width][None]
-    grad_value = owned[:, q_width + k_width : q_width + 2 * k_width][None]
-    grad_out = owned[:, q_width + 2 * k_width :][None]
+    grad_query = left_term[:, :q_width][None]
+    grad_key = left_term[:, q_width : q_width + k_width][None]
+    grad_value = left_term[:, q_width + k_width :][None]
+    grad_out = right_term[None]
     norm_term = first_slot[5] + second_slot[5]
     feature_count = norm_term.shape[0]
     half_width = feature_count // lax.axis_size("tensor")

time: 438 us -> 278 us (0.63)
  waiting for transfers between devices: 246 us -> 93.2 us
  other arithmetic: 18.4 us -> 7.51 us
  blocking collectives: 93.5 us -> 99.7 us
  starting transfers between devices: 4.7 us -> 9.36 us
  matrix products: 42.9 us -> 38.4 us
    reduce_scatter x1 -> x0, waiting for transfers between devices: 132 us -> none  [local(): lax.psum_scatter((jnp.concatenate([left_term, right_term], axis=1) * grad...]
    psum x2 -> x0, waiting for transfers between devices: 32.1 us -> none  [tensor_sums(): lax.psum(out_part.astype(jnp.bfloat16), 'tensor').astype(jnp.float32)]
    convert_element_type x5 -> x1, other arithmetic: 9.93 us -> 0.13 us  [run_slot(): d_input = (cot_rows.astype(jnp.float32) + unit_back(d_normed * norm_scale...]
    all_gather x0 -> x1, waiting for transfers between devices: none -> 6.72 us  [local(): lax.all_gather(jnp.concatenate([column_rows, attended_rows], axis=1), 'dp...]
    psum x1, blocking collectives: 29.9 us -> 36 us  [local(): lax.psum((own_half * grad_scale, qk_term * grad_scale), ('dp', 'tensor'))]
    all_to_all x0 -> x1, starting transfers between devices: none -> 4.6 us  [local(): lax.all_to_all(jnp.stack([normed_rows, cot_rows]), 'dp', split_axis=2, co...]
  transfers between devices with their start and end apart: 8 -> 9, of which waited for: 6 -> 6; matrix products, arithmetic and copies ran while one was open for 7% -> 12% of each run, Pallas kernels for 0% -> 0%
where the time goes in v1:
time: 278 us; the launch traced here: 276 us
  blocking collectives  99.7 us (36%)
  waiting for transfers between devices  93.2 us (34%)
  matrix products  38.4 us (14%)
  between operations  14.4 us (5%)
  local copies, waits for them, and re-layouts  13.3 us (5%)
  starting transfers between devices  9.36 us (3%)
  other arithmetic  7.51 us (3%)
    all_gather x1, waiting for transfers between devices, local(): lax.all_gather(w_out, 'dp', axis=1, tiled=True)  62.8 us
    psum x1, blocking collectives, local(): lax.psum((own_half * grad_scale, qk_term * grad_scale), ('dp', 'tensor'))  36 us
    all_gather x1, blocking collectives, local(): lax.all_gather(w_value, 'dp', axis=1, tiled=True)  33.2 us
    all_gather x1, blocking collectives, local(): lax.all_gather(w_key, 'dp', axis=1, tiled=True)  30.4 us
    all_gather x1, waiting for transfers between devices, local(): lax.all_gather(w_query, 'dp', axis=1, tiled=True)  16.2 us
    dot_general x4, matrix products, attend_local(): jnp.dot(normed, w_q, preferred_element_type=jnp.float32)  8.14 us
    dot_general x2, matrix products, backward_part(): lax.dot_general(q_grad, w_q, contract, preferred_element_type=jnp.float32)  7.36 us
    all_gather x1, waiting for transfers between devices, local(): lax.all_gather(jnp.concatenate([column_rows, attended_rows], axis=1), 'dp...  6.72 us
  transfers between devices with their start and end apart: 9, of which 6 were waited for; matrix products, arithmetic and copies ran while one was open for 12% of the time, Pallas kernels for 0%

profile of v1, /device:TPU:12, one launch (start us, length us, event | category | flops | bytes accessed | tf_op | source)
XLA Modules:
  0.0 275.8 jit_solution(16827082615793387058)
XLA Ops:
  7.2 0.7 all-gather.4.cloned.1.call-update
  7.9 0.7 all-gather.6.cloned.1.call-update
  8.7 0.6 collective-permute-start
  9.3 1.0 fusion.105
  10.3 30.4 %all_gather.16 = bf16[1,2048,128]{2,1,0:T(8,128)(2,1)S(1)} all-gather(bf16[1,256,128]{2,1,0:T(8,128)(2,1)} %param.19), channel_id=1, replica_groups=mesh['section'=2,'dp'=8,'tensor'=2] {'dp'}, dimensions={1}, use_global_device_ids=true | all-gather | bytes 589824 | tf_op jit(solution)/shard_map/all_gather | solution.py:215
  40.8 1.3 multiply_reduce_fusion.17
  42.1 0.8 slice_bitcast_fusion.4
  42.9 33.2 %all_gather.15 = bf16[1,2048,128]{2,1,0:T(8,128)(2,1)S(1)} all-gather(bf16[1,256,128]{2,1,0:T(8,128)(2,1)} %param.20), channel_id=1, replica_groups=mesh['section'=2,'dp'=8,'tensor'=2] {'dp'}, dimensions={1}, use_global_device_ids=true | all-gather | bytes 589824 | tf_op jit(solution)/shard_map/all_gather | solution.py:216
  76.3 1.0 fusion.47
  77.3 1.1 multiply_reduce_fusion.16
  78.5 16.2 %all-gather.4.cloned.1.call-done = bf16[1,2048,1024]{2,1,0:T(8,128)(2,1)} async-done(((bf16[1,256,1024]{2,1,0:T(8,128)(2,1)}), bf16[1,2048,1024]{2,1,0:T(8,128)(2,1)}) %all-gather.4.cloned.1.call-update) | async-done | bytes 4194320 | tf_op jit(solution)/shard_map/all_gather | solution.py:214
  94.8 6.5 %copy.66 = bf16[1024,2048]{1,0:T(8,128)(2,1)} copy(bf16[1024,2048]{0,1:T(8,128)(2,1)} %bitcast.485) | data formatting | bytes 8388608 | tf_op jit(solution)/shard_map/dot_general | solution.py:83
  101.2 3.8 %multiply_reduce_fusion.8 = (f32[32,8]{0,1:T(8,128)S(1)}, f32[32,8,128]{2,0,1:T(8,128)S(1)}) fusion(bf16[8,128,2048]{2,1,0:T(8,128)(2,1)} %bitcast.481, f32[2048]{0:T(1024)S(1)} %bitcast.492, f32[32]{0:T(128)S(1)} %add_rsqrt_fusion.9, bf16[2,32,2048]{2,1,0:T(8,128)(2,1)S(1)} %collective-permute-done), kind=kOutput, calls=%fused_computation.195 | convolution fusion | flops 134545152 | bytes 4466176 | tf_op jit(solution)/shard_map/dot_general | solution.py:83
  105.1 1.4 multiply_reduce_fusion.9
  107.2 62.8 %all-gather.6.cloned.1.call-done = bf16[1,2048,1024]{2,1,0:T(8,128)(2,1)} async-done(((bf16[1,256,1024]{2,1,0:T(8,128)(2,1)}), bf16[1,2048,1024]{2,1,0:T(8,128)(2,1)}) %all-gather.6.cloned.1.call-update) | async-done | bytes 4194320 | tf_op jit(solution)/shard_map/all_gather | solution.py:217
  169.9 3.0 %fusion.30 = bf16[32,1024]{1,0:T(8,128)(2,1)S(1)} fusion(bf16[1,2048,1024]{2,1,0:T(8,128)(2,1)} %all-gather.6.cloned.1.call-done, bf16[1,32,2048]{2,1,0:T(8,128)(2,1)S(1)} %copy-done.5), kind=kOutput, calls=%fused_computation.40 | convolution fusion | flops 134250496 | bytes 4390912 | tf_op jit(solution)/shard_map/dot_general | solution.py:131
  174.1 0.4 fusion.40
  175.5 3.8 %fusion.8 = f32[32,2048]{1,0:T(8,128)S(1)} fusion(bf16[1,2048,1024]{2,1,0:T(8,128)(2,1)} %all-gather.4.cloned.1.call-done, f32[32,8,128]{2,0,1:T(8,128)S(1)} %get-tuple-element.84, f32[32,8]{0,1:T(8,128)S(1)} %broadcast_multiply_fusion.1, f32[32,8]{0,1:T(8,128)S(1)} %add_rsqrt_fusion.2, f32[128]{0:T(128)S(1)} %get-tuple-element.67, ...), kind=kOutput, calls=%fused_computation.8 | convolution fusion | flops 134447104 | bytes 4721152 | tf_op jit(solution)/shard_map/dot_general | solution.py:159
  180.0 1.3 fusion.14
  181.9 1.1 collective-permute-done.1
  183.4 2.5 collective-permute-start.3
  185.9 1.5 collective-permute-start.2
  187.3 0.4 multiply_reduce_fusion.13
  187.7 1.4 multiply_reduce_fusion.4
  189.4 3.6 %collective-permute-done.2 = bf16[32,2048]{1,0:T(8,128)(2,1)S(1)} collective-permute-done((bf16[32,2048]{1,0:T(8,128)(2,1)S(1)}, bf16[32,2048]{1,0:T(8,128)(2,1)S(1)}, u32[]{:S(2)}, u32[]{:S(2)}) %collective-permute-start.2) | collective-permute-done | bytes 131104 | tf_op jit(solution)/shard_map/ppermute | solution.py:28
  193.2 1.5 multiply_reduce_fusion.5
  194.6 0.4 multiply_reduce_fusion.14
  195.5 0.3 fusion.199
  195.9 0.8 fusion.33
  198.9 3.5 %fusion.10 = f32[32,2048]{1,0:T(8,128)S(1)} fusion(bf16[1,2048,1024]{2,1,0:T(8,128)(2,1)} %all-gather.4.cloned.1.call-done, f32[32,8,128]{2,0,1:T(8,128)S(1)} %get-tuple-element.98, f32[32,8]{0,1:T(8,128)S(1)} %broadcast_multiply_fusion, f32[32,8]{0,1:T(8,128)S(1)} %get-tuple-element.111, f32[128]{0:T(128)S(1)} %get-tuple-element.67, ...), kind=kOutput, calls=%fused_computation.10 | convolution fusion | flops 134447104 | bytes 4721152 | tf_op jit(solution)/shard_map/dot_general | solution.py:159
  203.1 0.7 maximum_maximum_fusion
  203.8 0.3 fusion.200
  204.2 0.4 fusion.41
  204.6 3.5 %fusion.17 = bf16[32,2048]{1,0:T(8,128)(2,1)S(1)} fusion(bf16[1,2048,1024]{2,1,0:T(8,128)(2,1)} %all-gather.6.cloned.1.call-done, bf16[4,8,8,128]{3,2,1,0:T(8,128)(2,1)S(1)} %bitcast.513), kind=kOutput, calls=%fused_computation.20 | convolution fusion | flops 134283264 | bytes 4390912 | tf_op jit(solution)/shard_map/dot_general | solution.py:117
  208.3 1.5 collective-permute-done.4
  210.3 0.8 copy.79
  211.1 1.5 reshape.758
  212.6 4.6 %all-to-all-start = ((bf16[8,2,16384]{2,1,0:T(2,128)(2,1)}), bf16[8,2,16384]{2,1,0:T(2,128)(2,1)S(1)}, u32[]{:S(2)}, u32[]{:S(2)}) async-start(bf16[8,2,16384]{2,1,0:T(2,128)(2,1)} %reshape.758), calls=%async_computation | async-start | bytes 1048576 | tf_op jit(solution)/shard_map/all_to_all | solution.py:248
  217.2 36.0 %all-reduce = (f32[1,2048]{1,0:T(1,128)}, f32[1,2,128]{2,1,0:T(2,128)}) all-reduce(f32[1,2048]{1,0:T(1,128)S(1)} %bitcast.520, f32[1,2,128]{2,1,0:T(2,128)S(1)} %fusion.172), channel_id=1, replica_groups=mesh['section'=2,'dp'=8,'tensor'=2] {'dp','tensor'}, use_global_device_ids=true, to_apply=%region_26.27 | all-reduce | flops 2304 | bytes 18432 | tf_op jit(solution)/shard_map/psum | solution.py:275
  253.3 0.7 maximum_bitcast_fusion.1
  254.0 0.7 maximum_bitcast_fusion
  254.7 0.7 reshape.759
  255.4 0.7 copy.93
  256.2 6.7 %all-gather.8.cloned.1.call-done = bf16[512,2304]{1,0:T(8,128)(2,1)} async-done(((bf16[64,2304]{1,0:T(8,128)(2,1)}), bf16[512,2304]{1,0:T(8,128)(2,1)}) %all-gather.8.cloned.1.call-update) | async-done | bytes 2359312 | tf_op jit(solution)/shard_map/all_gather | solution.py:251
  263.0 1.8 convolution_multiply_fusion
  264.8 0.7 slice_bitcast_fusion.1
  265.5 1.1 slice_bitcast_fusion
  266.6 2.7 fusion.20
  (114 shorter events, 9.3 us)
Async XLA Ops:
  7.2 87.6 %all-gather.4.cloned.1.call-start = ((), (), s32[]{:S(2)}) async-start(), calls=%async_computation.1 | async-start | bytes 4718592 | tf_op jit(solution)/shard_map/all_gather | solution.py:214
  7.9 162.0 %all-gather.6.cloned.1.call-start = ((), (), s32[]{:S(2)}) async-start(), calls=%async_computation.2 | async-start | bytes 4718592 | tf_op jit(solution)/shard_map/all_gather | solution.py:217
  8.7 254.3 %all-gather.8.cloned.1.call-start = ((), (), s32[]{:S(2)}) async-start(), calls=%async_computation.3 | async-start | bytes 2654208 | tf_op jit(solution)/shard_map/all_gather | solution.py:251
  8.7 67.4 %collective-permute-start = (bf16[2,32,2048]{2,1,0:T(8,128)(2,1)}, bf16[2,32,2048]{2,1,0:T(8,128)(2,1)S(1)}, u32[]{:S(2)}, u32[]{:S(2)}) collective-permute-start(bf16[2,32,2048]{2,1,0:T(8,128)(2,1)} %bitcast.521), channel_id=1, source_target_pairs={{0,16},{16,0},{1,17},{17,1},{2,18},{18,2},{3,19},{19,3},{4,20},{20... | collective-permute-start | bytes 786440 | tf_op jit(solution)/shard_map/ppermute | solution.py:22
  94.8 6.5 %copy-start.4 = (f32[1,2048]{1,0:T(1,128)S(1)}, f32[1,2048]{1,0:T(1,128)}, u32[]{:S(2)}) copy-start(f32[1,2048]{1,0:T(1,128)} %param.16) | copy-start | bytes 24580
  101.2 3.8 %copy-start = (bf16[1024,2048]{1,0:T(8,128)(2,1)S(1)}, bf16[1024,2048]{1,0:T(8,128)(2,1)}, u32[]{:S(2)}) copy-start(bf16[1024,2048]{1,0:T(8,128)(2,1)} %copy.66) | copy-start | bytes 12582916
  101.2 3.8 %copy-start.3 = (bf16[1,32,2048]{2,1,0:T(8,128)(2,1)S(1)}, bf16[1,32,2048]{2,1,0:T(8,128)(2,1)}, u32[]{:S(2)}) copy-start(bf16[1,32,2048]{2,1,0:T(8,128)(2,1)} %param.11) | copy-start | bytes 393220
  101.2 68.7 %copy-start.5 = (bf16[1,32,2048]{2,1,0:T(8,128)(2,1)S(1)}, bf16[1,32,2048]{2,1,0:T(8,128)(2,1)}, u32[]{:S(2)}) copy-start(bf16[1,32,2048]{2,1,0:T(8,128)(2,1)} %param.13) | copy-start | bytes 393220
  175.0 4.9 %copy-start.2 = (bf16[1,2048,1024]{2,1,0:T(8,128)(2,1)S(1)}, bf16[1,2048,1024]{2,1,0:T(8,128)(2,1)}, u32[]{:S(2)}) copy-start(bf16[1,2048,1024]{2,1,0:T(8,128)(2,1)} %all-gather.6.cloned.1.call-done) | copy-start | bytes 12582916
  180.0 7.8 %copy-start.1 = (bf16[1024,2048]{1,0:T(8,128)(2,1)S(1)}, bf16[1024,2048]{1,0:T(8,128)(2,1)}, u32[]{:S(2)}) copy-start(bf16[1024,2048]{1,0:T(8,128)(2,1)} %copy.66) | copy-start | bytes 12582916
  181.3 1.6 collective-permute-start.1
  181.9 11.1 %copy-start.6 = (bf16[32,2048]{1,0:T(8,128)(2,1)S(1)}, bf16[32,2048]{1,0:T(8,128)(2,1)}, u32[]{:S(2)}) copy-start(bf16[32,2048]{1,0:T(8,128)(2,1)} %param.12) | copy-start | bytes 393220
  183.4 12.4 %collective-permute-start.3 = (bf16[32,2048]{1,0:T(8,128)(2,1)S(1)}, bf16[32,2048]{1,0:T(8,128)(2,1)S(1)}, u32[]{:S(2)}, u32[]{:S(2)}) collective-permute-start(bf16[32,2048]{1,0:T(8,128)(2,1)S(1)} %fusion.89), channel_id=1, source_target_pairs={{16,0},{17,1},{18,2},{19,3},{20,4},{21,5},{22,6},{23,7},{24,8},{25... | collective-permute-start | bytes 393224 | tf_op jit(solution)/shard_map/ppermute | solution.py:28
  185.9 7.2 %collective-permute-start.2 = (bf16[32,2048]{1,0:T(8,128)(2,1)S(1)}, bf16[32,2048]{1,0:T(8,128)(2,1)S(1)}, u32[]{:S(2)}, u32[]{:S(2)}) collective-permute-start(bf16[32,2048]{1,0:T(8,128)(2,1)S(1)} %get-tuple-element.31), channel_id=1, source_target_pairs={{0,16},{1,17},{2,18},{3,19},{4,20},{5,21},{6,22},{7,23},{8,24},{9,... | collective-permute-start | bytes 393224 | tf_op jit(solution)/shard_map/ppermute | solution.py:28
  189.2 6.7 %copy-start.7 = (bf16[32,2048]{1,0:T(8,128)(2,1)S(1)}, bf16[32,2048]{1,0:T(8,128)(2,1)}, u32[]{:S(2)}) copy-start(bf16[32,2048]{1,0:T(8,128)(2,1)} %param.14) | copy-start | bytes 393220
  208.2 1.6 collective-permute-start.4
  212.6 42.1 %all-to-all-start = ((bf16[8,2,16384]{2,1,0:T(2,128)(2,1)}), bf16[8,2,16384]{2,1,0:T(2,128)(2,1)S(1)}, u32[]{:S(2)}, u32[]{:S(2)}) async-start(bf16[8,2,16384]{2,1,0:T(2,128)(2,1)} %reshape.758), calls=%async_computation | async-start | bytes 1048576 | tf_op jit(solution)/shard_map/all_to_all | solution.py:248
Sparse Core Ops, SparseCore 0:
  10.1 84.5 all-gather.3
  96.9 73.0 all-gather.5
  204.0 58.9 all-gather.7

commit v2 on v1

--- a/solution.py
+++ b/solution.py
@@ -1,8 +1,11 @@
+import functools
 import math
 
 import jax
 import jax.numpy as jnp
 from jax import lax
+from jax.experimental import pallas as pl
+from jax.experimental.pallas import tpu as pltpu
 from jax.sharding import PartitionSpec as P
 
 HD = 128
@@ -26,6 +29,189 @@
     count = lax.axis_size(axis)
     pairs = [(i, i + by) for i in range(count) if 0 <= i + by < count]
     return lax.ppermute(array, axis, pairs)
+
+
+def grid_of(count):
+    tall = 4 if count % 4 == 0 else 1
+    return tall, count // tall
+
+
+def meet(peers):
+    barrier = pltpu.get_barrier_semaphore()
+    for peer in peers:
+        pl.semaphore_signal(barrier, inc=1, device_id=peer)
+    pl.semaphore_wait(barrier, len(peers))
+
+
+class Sends:
+    def __init__(self, sems):
+        self.sems = sems
+        self.started = []
+
+    def start(self, src, dst, recv, peer):
+        copy = pltpu.make_async_remote_copy(
+            src_ref=src,
+            dst_ref=dst,
+            send_sem=self.sems.at[len(self.started)],
+            recv_sem=recv,
+            device_id=peer,
+        )
+        copy.start()
+        self.started.append(copy)
+
+    def arrived(self, dst, recv, peer):
+        pltpu.make_async_remote_copy(
+            src_ref=dst, dst_ref=dst, send_sem=self.sems.at[0], recv_sem=recv, device_id=peer
+        ).wait_recv()
+
+    def finish(self):
+        for copy in self.started:
+            copy.wait_send()
+
+
+def neighbours(count):
+    tall, wide = grid_of(count)
+    me = lax.axis_index("dp")
+    row, col = me // wide, me % wide
+    across = [row * wide + (col + i) % wide for i in range(1, wide)]
+    along = [((row + i) % tall) * wide + col for i in range(1, tall)]
+    return me, row, across, along
+
+
+def spread(sends, pieces, me, across, along, recv):
+    for c, (src, dst) in enumerate(pieces):
+        for peer in along + across:
+            sends.start(src, dst(me), recv.at[me, c], {"dp": peer})
+
+
+def relay(sends, pieces, c, across, along, recv):
+    dst = pieces[c][1]
+    for peer in along:
+        sends.arrived(dst(peer), recv.at[peer, c], {"dp": peer})
+        for other in across:
+            sends.start(dst(peer), dst(peer), recv.at[peer, c], {"dp": other})
+
+
+def collect(sends, pieces, c, row, count, across, recv):
+    tall, wide = grid_of(count)
+    dst = pieces[c][1]
+    for other in across:
+        for i in range(tall):
+            shard = ((row + i) % tall) * wide + other % wide
+            sends.arrived(dst(shard), recv.at[shard, c], {"dp": other})
+
+
+def halves(src, full, depth):
+    half = depth // 2
+    return [
+        (src.at[pl.ds(i * half, half)], lambda j, i=i: full.at[j, pl.ds(i * half, half)])
+        for i in range(2)
+    ]
+
+
+def weights_kernel(count, in_ref, out_ref, full_in, full_out, send, recv, own):
+    me, row, across, along = neighbours(count)
+    depth = in_ref.shape[0]
+    meet([{"dp": j} for j in along + across])
+    pieces = halves(in_ref, full_in, depth) + halves(out_ref, full_out, depth)
+    sends = Sends(send)
+    spread(sends, pieces, me, across, along, recv)
+    mine = [
+        pltpu.make_async_copy(in_ref, full_in.at[me], own.at[0]),
+        pltpu.make_async_copy(out_ref, full_out.at[me], own.at[1]),
+    ]
+    for copy in mine:
+        copy.start()
+    for c in range(len(pieces)):
+        relay(sends, pieces, c, across, along, recv)
+    for c in range(len(pieces)):
+        collect(sends, pieces, c, row, count, across, recv)
+    for copy in mine:
+        copy.wait()
+    sends.finish()
+
+
+def grads_kernel(count, cols_ref, acts_ref, small_ref, full, sliced, smalls, send, recv, own):
+    me, row, across, along = neighbours(count)
+    core = lax.axis_index("tensor")
+    depth = sliced.shape[-1]
+    everyone = [{"dp": (me + i) % count} for i in range(1, count)]
+    crossed = [{"dp": (me + i) % count, "tensor": 1 - core} for i in range(count)]
+    meet(everyone + crossed)
+    pieces = halves(cols_ref, full, cols_ref.shape[0])
+    sends = Sends(send)
+    spread(sends, pieces, me, across, along, recv)
+    for peer in everyone:
+        block = pl.ds(pl.multiple_of(peer["dp"] * depth, depth), depth)
+        sends.start(acts_ref.at[:, :, block], sliced.at[me], recv.at[me, 2], peer)
+    for peer in everyone + crossed:
+        sends.start(small_ref, smalls.at[core, me], recv.at[me, 3 + core], peer)
+    block = pl.ds(pl.multiple_of(me * depth, depth), depth)
+    mine = [
+        pltpu.make_async_copy(cols_ref, full.at[me], own.at[0]),
+        pltpu.make_async_copy(acts_ref.at[:, :, block], sliced.at[me], own.at[1]),
+        pltpu.make_async_copy(small_ref, smalls.at[core, me], own.at[2]),
+    ]
+    for copy in mine:
+        copy.start()
+    for c in range(2):
+        relay(sends, pieces, c, across, along, recv)
+    for c in range(2):
+        collect(sends, pieces, c, row, count, across, recv)
+    for peer in everyone:
+        j = peer["dp"]
+        sends.arrived(sliced.at[j], recv.at[j, 2], peer)
+        sends.arrived(smalls.at[core, j], recv.at[j, 3 + core], peer)
+    for peer in crossed:
+        j = peer["dp"]
+        sends.arrived(smalls.at[1 - core, j], recv.at[j, 4 - core], peer)
+    for copy in mine:
+        copy.wait()
+    sends.finish()
+
+
+ANY = pl.BlockSpec(memory_space=pl.ANY)
+
+
+def gather_weights(w_in, w_out):
+    count = lax.axis_size("dp")
+    tall, wide = grid_of(count)
+    sent = 4 * (tall + wide - 2 + (tall - 1) * (wide - 1))
+    return pl.pallas_call(
+        functools.partial(weights_kernel, count),
+        out_shape=[jax.ShapeDtypeStruct((count,) + w.shape, w.dtype) for w in (w_in, w_out)],
+        in_specs=[ANY] * 2,
+        out_specs=[ANY] * 2,
+        scratch_shapes=[
+            pltpu.SemaphoreType.DMA((sent,)),
+            pltpu.SemaphoreType.DMA((count, 4)),
+            pltpu.SemaphoreType.DMA((2,)),
+        ],
+        compiler_params=pltpu.CompilerParams(collective_id=0, has_side_effects=True),
+    )(w_in, w_out)
+
+
+def exchange_grads(cols, acts, small):
+    count = lax.axis_size("dp")
+    tall, wide = grid_of(count)
+    rows, width = acts.shape[1:]
+    sent = 2 * (tall + wide - 2 + (tall - 1) * (wide - 1)) + 3 * count - 2
+    return pl.pallas_call(
+        functools.partial(grads_kernel, count),
+        out_shape=[
+            jax.ShapeDtypeStruct((count,) + cols.shape, cols.dtype),
+            jax.ShapeDtypeStruct((count, 2, rows, width // count), acts.dtype),
+            jax.ShapeDtypeStruct((2, count) + small.shape, small.dtype),
+        ],
+        in_specs=[ANY] * 3,
+        out_specs=[ANY] * 3,
+        scratch_shapes=[
+            pltpu.SemaphoreType.DMA((sent,)),
+            pltpu.SemaphoreType.DMA((count, 5)),
+            pltpu.SemaphoreType.DMA((3,)),
+        ],
+        compiler_params=pltpu.CompilerParams(collective_id=1, has_side_effects=True),
+    )(cols, acts, small)
 
 
 def rope_tables(length, width):
@@ -210,13 +396,20 @@
     w_value,
     w_out,
 ):
-    full_q, full_k, full_v, full_o = (
-        lax.all_gather(w_query, "dp", axis=1, tiled=True),
-        lax.all_gather(w_key, "dp", axis=1, tiled=True),
-        lax.all_gather(w_value, "dp", axis=1, tiled=True),
-        lax.all_gather(w_out, "dp", axis=1, tiled=True),
-    )
-    weights = (full_q[0], full_k[0], full_v[0], full_o[0])
+    q_width = w_query.shape[2]
+    k_width = w_key.shape[2]
+    left_width = q_width + 2 * k_width
+    full_in, full_o = gather_weights(
+        jnp.concatenate([w_query[0], w_key[0], w_value[0]], axis=1), w_out[0]
+    )
+    full_in = full_in.reshape(-1, left_width)
+    full_o = full_o.reshape(-1, w_out.shape[2])
+    weights = (
+        full_in[:, :q_width],
+        full_in[:, q_width : q_width + k_width],
+        full_in[:, q_width + k_width :],
+        full_o,
+    )
     norm_scale = norm_gain[0]
     qk_gains = qk_gain[0]
     row_count = fwd_input.shape[1]
@@ -245,13 +438,21 @@
     cot_rows = jnp.concatenate([cotangent[0], second_cot], axis=0)
     attended_rows = jnp.concatenate([first_slot[4], second_slot[4]], axis=0)
     contract = (((0,), (0,)), ((), ()))
-    sliced = lax.all_to_all(
-        jnp.stack([normed_rows, cot_rows]), "dp", split_axis=2, concat_axis=1, tiled=True
-    )
-    gathered = lax.all_gather(
-        jnp.concatenate([column_rows, attended_rows], axis=1), "dp", axis=0, tiled=True
-    )
-    left_width = column_rows.shape[1]
+    norm_term = first_slot[5] + second_slot[5]
+    qk_term = jnp.stack([first_slot[6] + second_slot[6], first_slot[7] + second_slot[7]])
+    feature_rows = norm_term.shape[0] // HD
+    small = jnp.concatenate(
+        [norm_term.reshape(feature_rows, HD), qk_term, jnp.zeros((6, HD), jnp.float32)], axis=0
+    )
+    gathered, sliced, smalls = exchange_grads(
+        jnp.concatenate([column_rows, attended_rows], axis=1),
+        jnp.stack([normed_rows, cot_rows]),
+        small * grad_scale,
+    )
+    gathered = gathered.reshape(-1, gathered.shape[-1])
+    sliced = jnp.moveaxis(sliced, 1, 0).reshape(2, -1, sliced.shape[-1])
+    norm_total = jnp.sum(smalls[0, :, :feature_rows], axis=0).reshape(-1)
+    qk_total = jnp.sum(smalls[:, :, feature_rows : feature_rows + 2], axis=(0, 1))
     left_term = lax.dot_general(
         sliced[0], gathered[:, :left_width], contract, preferred_element_type=jnp.float32
     )
@@ -260,19 +461,10 @@
     )
     left_term = left_term * grad_scale
     right_term = right_term * grad_scale
-    q_width = w_query.shape[2]
-    k_width = w_key.shape[2]
     grad_query = left_term[:, :q_width][None]
     grad_key = left_term[:, q_width : q_width + k_width][None]
     grad_value = left_term[:, q_width + k_width :][None]
     grad_out = right_term[None]
-    norm_term = first_slot[5] + second_slot[5]
-    feature_count = norm_term.shape[0]
-    half_width = feature_count // lax.axis_size("tensor")
-    feature_owner = lax.broadcasted_iota(jnp.int32, (feature_count,), 0) // half_width
-    own_half = jnp.where(feature_owner == lax.axis_index("tensor"), norm_term, 0.0)
-    qk_term = jnp.stack([first_slot[6] + second_slot[6], first_slot[7] + second_slot[7]])
-    norm_total, qk_total = lax.psum((own_half * grad_scale, qk_term * grad_scale), ("dp", "tensor"))
     return (
         out_activations,
         grad_input,

time: 278 us -> 279 us (level)
  Pallas kernels: 0 us -> 191 us
  blocking collectives: 99.7 us -> 0 us
  waiting for transfers between devices: 93.2 us -> 5.04 us
  between operations: 14.4 us -> 1.37 us
  matrix products: 38.4 us -> 46.9 us
  other arithmetic: 7.51 us -> 13.2 us
  starting transfers between devices: 9.36 us -> 5.62 us
    pallas_call x0 -> x2, Pallas kernels: none -> 191 us  [the longest x1 140 us: gather_weights(): pl.pallas_call(functools.partial(weights_kernel, count), out_shape=[jax.S...]
    all_gather x3 -> x0, waiting for transfers between devices: 85.7 us -> none  [the longest x1 62.8 us: local(): lax.all_gather(w_out, 'dp', axis=1, tiled=True)]
    all_gather x2 -> x0, blocking collectives: 63.6 us -> none  [the longest x1 33.2 us: local(): lax.all_gather(w_value, 'dp', axis=1, tiled=True)]
    psum x1 -> x0, blocking collectives: 36 us -> none  [local(): lax.psum((own_half * grad_scale, qk_term * grad_scale), ('dp', 'tensor'))]
    dot_general x1 -> x2, local copies, waits for them, and re-layouts: 6.47 us -> 11.2 us  [attend_local(): jnp.dot(normed, w_q, preferred_element_type=jnp.float32)]
    all_to_all x1 -> x0, starting transfers between devices: 4.6 us -> none  [local(): lax.all_to_all(jnp.stack([normed_rows, cot_rows]), 'dp', split_axis=2, co...]
    reduce_sum x0 -> x3, other arithmetic: none -> 2.98 us  [the longest x1 1.45 us: local(): norm_total = jnp.sum(smalls[0, :, :feature_rows], axis=0).reshape(-1)]
  transfers between devices with their start and end apart: 9 -> 5, of which waited for: 6 -> 2; matrix products, arithmetic and copies ran while one was open for 12% -> 9% of each run, Pallas kernels for 0% -> 50%
where the time goes in v2:
time: 279 us; the launch traced here: 278 us
  Pallas kernels  191 us (68%)
  matrix products  46.9 us (17%)
  local copies, waits for them, and re-layouts  14.8 us (5%)
  other arithmetic  13.2 us (5%)
  starting transfers between devices  5.62 us (2%)
  waiting for transfers between devices  5.04 us (2%)
    pallas_call x1, Pallas kernels, gather_weights(): pl.pallas_call(functools.partial(weights_kernel, count), out_shape=[jax.S...  140 us
    pallas_call x1, Pallas kernels, exchange_grads(): pl.pallas_call(functools.partial(grads_kernel, count), out_shape=[jax.Sha...  50.9 us
    dot_general x2, local copies, waits for them, and re-layouts, attend_local(): jnp.dot(normed, w_q, preferred_element_type=jnp.float32)  11.2 us
    dot_general x4, matrix products, attend_local(): jnp.dot(normed, w_q, preferred_element_type=jnp.float32)  9.75 us
    dot_general x2, matrix products, backward_part(): lax.dot_general(q_grad, w_q, contract, preferred_element_type=jnp.float32)  7.21 us
    dot_general x2, matrix products, forward_part(): lax.dot_general(attended, w_o, (((1,), (1,)), ((), ())), preferred_elemen...  7.11 us
  transfers between devices with their start and end apart: 5, of which 2 were waited for; matrix products, arithmetic and copies ran while one was open for 9% of the time, Pallas kernels for 50%

profile of v2, /device:TPU:12, one launch (start us, length us, event | category | flops | bytes accessed | tf_op | source)
XLA Modules:
  0.0 278.1 jit_solution(7508067037643144205)
XLA Ops:
  0.6 0.6 collective-permute-start
  1.2 2.0 pad_maximum_fusion.in_ref
  3.2 140.3 %shard_map.170 = (bf16[8,256,1280]{2,1,0:T(8,128)(2,1)}, bf16[8,256,1024]{2,1,0:T(8,128)(2,1)}) custom-call(bf16[256,1280]{1,0:T(8,128)(2,1)} %pad_maximum_fusion.in_ref, bf16[256,1024]{1,0:T(8,128)(2,1)} %bitcast.477), custom_call_target="tpu_custom_call" | custom-call | tf_op jit(solution)/shard_map/pallas_call | solution.py:180
  143.6 4.7 %slice_bitcast_fusion = bf16[1024,2048]{0,1:T(8,128)(2,1)} fusion(bf16[2048,1280]{1,0:T(8,128)(2,1)} %bitcast.439), kind=kLoop, calls=%fused_computation.7 | loop fusion | bytes 8388608 | tf_op jit(solution)/shard_map/dot_general | solution.py:269
  148.3 6.5 %copy.76 = bf16[1024,2048]{1,0:T(8,128)(2,1)} copy(bf16[1024,2048]{0,1:T(8,128)(2,1)} %slice_bitcast_fusion) | data formatting | bytes 8388608 | tf_op jit(solution)/shard_map/dot_general | solution.py:269
  155.0 3.8 %multiply_reduce_fusion.9 = (f32[32,8]{0,1:T(8,128)S(1)}, f32[32,8,128]{2,0,1:T(8,128)S(1)}) fusion(bf16[8,128,2048]{2,1,0:T(8,128)(2,1)} %bitcast.436, bf16[1,32,2048]{2,1,0:T(8,128)(2,1)S(1)} %copy-done.3, f32[2048]{0:T(1024)S(1)} %bitcast.462, f32[32]{0:T(128)S(1)} %add_rsqrt_fusion.11), kind=kOutput, calls=%fused_computation.194 | convolution fusion | flops 134545152 | bytes 4465792 | tf_op jit(solution)/shard_map/dot_general | solution.py:269
  158.9 0.8 convolution_convert_fusion.2
  159.9 1.4 multiply_reduce_fusion.17
  161.6 1.4 multiply_reduce_fusion.16
  162.9 1.2 fusion.29
  164.2 3.6 %multiply_reduce_fusion.8 = (f32[32,8]{0,1:T(8,128)S(1)}, f32[32,8,128]{2,0,1:T(8,128)S(1)}) fusion(bf16[8,128,2048]{2,1,0:T(8,128)(2,1)} %bitcast.437, f32[32]{0:T(128)S(1)} %add_rsqrt_fusion.9, f32[2048]{0:T(1024)S(1)} %bitcast.465, bf16[2,32,2048]{2,1,0:T(8,128)(2,1)S(1)} %collective-permute-done), kind=kOutput, calls=%fused_computation.188 | convolution fusion | flops 134545152 | bytes 4466176 | tf_op jit(solution)/shard_map/dot_general | solution.py:269
  168.3 0.3 fusion.173
  169.4 0.3 fusion.174
  169.8 1.5 fusion.22
  171.3 3.6 %convolution_convert_fusion.1 = bf16[32,2048]{1,0:T(8,128)(2,1)S(1)} fusion(bf16[2048,1024]{1,0:T(8,128)(2,1)} %bitcast.432, bf16[4,8,8,128]{3,2,1,0:T(8,128)(2,1)S(1)} %bitcast.485), kind=kOutput, calls=%fused_computation.15 | convolution fusion | flops 134283264 | bytes 4390912 | tf_op jit(solution)/shard_map/dot_general | solution.py:303
  175.7 3.7 %fusion.4 = f32[32,2048]{1,0:T(8,128)S(1)} fusion(bf16[2048,1280]{1,0:T(8,128)(2,1)} %bitcast.444, f32[32,8,128]{2,0,1:T(8,128)S(1)} %get-tuple-element.92, f32[32,8]{0,1:T(8,128)S(1)} %broadcast_multiply_fusion.1, f32[32,8]{0,1:T(8,128)S(1)} %add_rsqrt_fusion.2, f32[128]{0:T(128)S(1)} %get-tuple-element.75, f32[32,8,64]{2,0,1:T(8,128)S(1)} %get-tuple-element.51, ...), kind=kOutput, calls=%fused_computation.5 | convolution fusion | flops 134447104 | bytes 4721152 | tf_op jit(solution)/shard_map/dot_general | solution.py:345
  179.5 1.5 convolution_add_fusion.3
  181.0 1.3 fusion.6
  182.9 1.1 collective-permute-done.1
  184.1 0.2 fusion.56
  184.5 0.3 multiply_reduce_fusion.13
  184.8 3.4 %collective-permute-start.3 = (bf16[32,2048]{1,0:T(8,128)(2,1)S(1)}, bf16[32,2048]{1,0:T(8,128)(2,1)S(1)}, u32[]{:S(2)}, u32[]{:S(2)}) collective-permute-start(bf16[32,2048]{1,0:T(8,128)(2,1)S(1)} %get-tuple-element.40), channel_id=1, source_target_pairs={{16,0},{17,1},{18,2},{19,3},{20,4},{21,5},{22,6},{23,7},{24,8},{25... | collective-permute-start | bytes 393224 | tf_op jit(solution)/shard_map/ppermute | solution.py:31
  188.3 1.5 collective-permute-start.2
  189.8 1.4 multiply_reduce_fusion.4
  191.5 4.0 %collective-permute-done.2 = bf16[32,2048]{1,0:T(8,128)(2,1)S(1)} collective-permute-done((bf16[32,2048]{1,0:T(8,128)(2,1)S(1)}, bf16[32,2048]{1,0:T(8,128)(2,1)S(1)}, u32[]{:S(2)}, u32[]{:S(2)}) %collective-permute-start.2) | collective-permute-done | bytes 131104 | tf_op jit(solution)/shard_map/ppermute | solution.py:31
  195.6 0.9 fusion.2
  196.5 0.4 multiply_reduce_fusion.14
  196.9 0.8 convolution_convert_fusion.5
  198.5 0.3 fusion.175
  199.9 3.5 %fusion = f32[32,2048]{1,0:T(8,128)S(1)} fusion(bf16[2048,1280]{1,0:T(8,128)(2,1)} %bitcast.447, f32[32,8,128]{2,0,1:T(8,128)S(1)} %get-tuple-element.106, f32[32,8]{0,1:T(8,128)S(1)} %broadcast_multiply_fusion, f32[32,8]{0,1:T(8,128)S(1)} %add_rsqrt_fusion, f32[128]{0:T(128)S(1)} %get-tuple-element.75, f32[32,8,64]{2,0,1:T(8,128)S(1)} %get-tuple-element.45, ...), kind=kOutput, calls=%fused_computation.1 | convolution fusion | flops 134447104 | bytes 4721152 | tf_op jit(solution)/shard_map/dot_general | solution.py:345
  204.0 0.3 fusion.176
  204.3 1.5 fusion.23
  205.8 3.5 %convolution_convert_fusion = bf16[32,2048]{1,0:T(8,128)(2,1)S(1)} fusion(bf16[2048,1024]{1,0:T(8,128)(2,1)} %bitcast.433, bf16[4,8,8,128]{3,2,1,0:T(8,128)(2,1)S(1)} %bitcast.484), kind=kOutput, calls=%fused_computation.14 | convolution fusion | flops 134283264 | bytes 4390912 | tf_op jit(solution)/shard_map/dot_general | solution.py:303
  209.9 1.3 convolution_add_fusion.1
  211.2 1.3 fusion.7
  212.7 0.7 maximum_maximum_fusion.cols_ref
  213.5 0.8 pad_maximum_fusion.1.acts_ref
  214.6 0.7 maximum_multiply_fusion.small_ref
  215.3 50.9 %shard_map.171 = (bf16[8,64,2304]{2,1,0:T(8,128)(2,1)}, bf16[8,2,64,256]{3,2,1,0:T(8,128)(2,1)}, f32[2,8,24,128]{3,2,1,0:T(8,128)}) custom-call(bf16[64,2304]{1,0:T(8,128)(2,1)} %maximum_maximum_fusion.cols_ref, bf16[2,64,2048]{2,1,0:T(8,128)(2,1)} %pad_maximum_fusion.1.acts_ref, f32[24,128]{1,0:T(8,128)} %maximum_multiply_fusion.small_ref), custom_call_target="tpu_custom_call" | custom-call | tf_op jit(solution)/shard_map/pallas_call | solution.py:199
  266.2 1.1 fusion.172
  267.3 1.8 convolution_multiply_fusion
  269.2 1.1 slice_bitcast_fusion.1
  270.3 0.7 slice_bitcast_fusion.2
  271.0 1.4 slice_reduce_fusion
  272.4 1.4 slice_reduce_fusion.1
  273.9 2.7 fusion.8
  276.7 0.7 maximum_bitcast_fusion.1
  277.4 0.7 maximum_bitcast_fusion
  (114 shorter events, 7.5 us)
Async XLA Ops:
  0.6 160.7 %collective-permute-start = (bf16[2,32,2048]{2,1,0:T(8,128)(2,1)}, bf16[2,32,2048]{2,1,0:T(8,128)(2,1)S(1)}, u32[]{:S(2)}, u32[]{:S(2)}) collective-permute-start(bf16[2,32,2048]{2,1,0:T(8,128)(2,1)} %bitcast.496), channel_id=1, source_target_pairs={{0,16},{16,0},{1,17},{17,1},{2,18},{18,2},{3,19},{19,3},{4,20},{20... | collective-permute-start | bytes 786440 | tf_op jit(solution)/shard_map/ppermute | solution.py:25
  148.3 6.5 %copy-start.3 = (bf16[1,32,2048]{2,1,0:T(8,128)(2,1)S(1)}, bf16[1,32,2048]{2,1,0:T(8,128)(2,1)}, u32[]{:S(2)}) copy-start(bf16[1,32,2048]{2,1,0:T(8,128)(2,1)} %param.11) | copy-start | bytes 393220
  148.3 6.7 %copy-start.5 = (f32[1,2048]{1,0:T(1,128)S(1)}, f32[1,2048]{1,0:T(1,128)}, u32[]{:S(2)}) copy-start(f32[1,2048]{1,0:T(1,128)} %param.16) | copy-start | bytes 24580
  154.8 4.0 %copy-start.8 = (f32[1,2,128]{2,1,0:T(2,128)S(1)}, f32[1,2,128]{2,1,0:T(2,128)}, u32[]{:S(2)}) copy-start(f32[1,2,128]{2,1,0:T(2,128)} %param.17) | copy-start | bytes 3076
  154.8 4.1 %copy-start = (bf16[8,256,1024]{2,1,0:T(8,128)(2,1)S(1)}, bf16[8,256,1024]{2,1,0:T(8,128)(2,1)}, u32[]{:S(2)}) copy-start(bf16[8,256,1024]{2,1,0:T(8,128)(2,1)} %get-tuple-element.14) | copy-start | bytes 12582916
  154.8 4.1 %copy-start.4 = (bf16[1,32,2048]{2,1,0:T(8,128)(2,1)S(1)}, bf16[1,32,2048]{2,1,0:T(8,128)(2,1)}, u32[]{:S(2)}) copy-start(bf16[1,32,2048]{2,1,0:T(8,128)(2,1)} %param.13) | copy-start | bytes 393220
  171.3 13.2 %slice-start = ((s8[5242880]{0:T(1024)(128)(4,1)}), s8[1048576]{0:T(1024)(128)(4,1)S(1)}, s32[]{:S(2)}) async-start(s8[5242880]{0:T(1024)(128)(4,1)} %bitcast.451), calls=%async_computation | async-start | bytes 2097152
  175.7 8.8 %slice-start.1 = ((s8[5242880]{0:T(1024)(128)(4,1)}), s8[4194304]{0:T(1024)(128)(4,1)S(1)}, s32[]{:S(2)}) async-start(s8[5242880]{0:T(1024)(128)(4,1)} %bitcast.451), calls=%async_computation.1 | async-start | bytes 8388608
  179.3 10.4 %copy-start.2 = (bf16[1024,2048]{1,0:T(8,128)(2,1)S(1)}, bf16[1024,2048]{1,0:T(8,128)(2,1)}, u32[]{:S(2)}) copy-start(bf16[1024,2048]{1,0:T(8,128)(2,1)} %copy.76) | copy-start | bytes 12582916
  182.4 1.6 collective-permute-start.1
  184.1 11.4 %copy-start.6 = (bf16[32,2048]{1,0:T(8,128)(2,1)S(1)}, bf16[32,2048]{1,0:T(8,128)(2,1)}, u32[]{:S(2)}) copy-start(bf16[32,2048]{1,0:T(8,128)(2,1)} %param.12) | copy-start | bytes 393220
  184.8 12.0 %collective-permute-start.3 = (bf16[32,2048]{1,0:T(8,128)(2,1)S(1)}, bf16[32,2048]{1,0:T(8,128)(2,1)S(1)}, u32[]{:S(2)}, u32[]{:S(2)}) collective-permute-start(bf16[32,2048]{1,0:T(8,128)(2,1)S(1)} %get-tuple-element.40), channel_id=1, source_target_pairs={{16,0},{17,1},{18,2},{19,3},{20,4},{21,5},{22,6},{23,7},{24,8},{25... | collective-permute-start | bytes 393224 | tf_op jit(solution)/shard_map/ppermute | solution.py:31
  188.3 7.2 %collective-permute-start.2 = (bf16[32,2048]{1,0:T(8,128)(2,1)S(1)}, bf16[32,2048]{1,0:T(8,128)(2,1)S(1)}, u32[]{:S(2)}, u32[]{:S(2)}) collective-permute-start(bf16[32,2048]{1,0:T(8,128)(2,1)S(1)} %get-tuple-element.39), channel_id=1, source_target_pairs={{0,16},{1,17},{2,18},{3,19},{4,20},{5,21},{6,22},{7,23},{8,24},{9,... | collective-permute-start | bytes 393224 | tf_op jit(solution)/shard_map/ppermute | solution.py:31
  191.2 5.6 %copy-start.7 = (bf16[32,2048]{1,0:T(8,128)(2,1)S(1)}, bf16[32,2048]{1,0:T(8,128)(2,1)}, u32[]{:S(2)}) copy-start(bf16[32,2048]{1,0:T(8,128)(2,1)} %param.14) | copy-start | bytes 393220
  191.3 5.7 %copy-start.1 = (bf16[8,256,1024]{2,1,0:T(8,128)(2,1)S(1)}, bf16[8,256,1024]{2,1,0:T(8,128)(2,1)}, u32[]{:S(2)}) copy-start(bf16[8,256,1024]{2,1,0:T(8,128)(2,1)} %get-tuple-element.14) | copy-start | bytes 12582916
  212.6 1.8 collective-permute-start.4

commit v3 on v2

v3 whole, which is shorter than its diff:
```python
import functools
import math

import jax
import jax.numpy as jnp
from jax import lax
from jax.experimental import pallas as pl
from jax.experimental.pallas import tpu as pltpu
from jax.sharding import PartitionSpec as P

HD = 128


EPSILON = 1e-06
THETA = 1000000.0


def swapped(block, axis, apart):
    count = lax.axis_size(axis)
    route = []
    for low in range(count):
        high = low | 1 << apart
        if high != low and high < count:
            route += [(low, high), (high, low)]
    return lax.ppermute(block, axis, route)


def passed_along(array, axis, by):
    count = lax.axis_size(axis)
    pairs = [(i, i + by) for i in range(count) if 0 <= i + by < count]
    return lax.ppermute(array, axis, pairs)


def grid_of(count):
    tall = 4 if count % 4 == 0 else 1
    return tall, count // tall


def meet(peers):
    barrier = pltpu.get_barrier_semaphore()
    for peer in peers:
        pl.semaphore_signal(barrier, inc=1, device_id=peer)
    pl.semaphore_wait(barrier, len(peers))


class Sends:
    def __init__(self, sems):
        self.sems = sems
        self.started = []

    def start(self, src, dst, recv, peer):
        copy = pltpu.make_async_remote_copy(
            src_ref=src,
            dst_ref=dst,
            send_sem=self.sems.at[len(self.started)],
            recv_sem=recv,
            device_id=peer,
        )
        copy.start()
        self.started.append(copy)

    def arrived(self, dst, recv, peer):
        pltpu.make_async_remote_copy(
            src_ref=dst, dst_ref=dst, send_sem=self.sems.at[0], recv_sem=recv, device_id=peer
        ).wait_recv()

    def finish(self):
        for copy in self.started:
            copy.wait_send()


def neighbours(count):
    tall, wide = grid_of(count)
    me = lax.axis_index("dp")
    row, col = me // wide, me % wide
    across = [row * wide + (col + i) % wide for i in range(1, wide)]
    along = [((row + i) % tall) * wide + col for i in range(1, tall)]
    return me, row, across, along


def spread(sends, pieces, me, across, along, recv):
    for c, (src, dst) in enumerate(pieces):
        for peer in along + across:
            sends.start(src, dst(me), recv.at[me, c], {"dp": peer})


def relay(sends, pieces, c, across, along, recv):
    dst = pieces[c][1]
    for peer in along:
        sends.arrived(dst(peer), recv.at[peer, c], {"dp": peer})
        for other in across:
            sends.start(dst(peer), dst(peer), recv.at[peer, c], {"dp": other})


def collect(sends, pieces, c, row, count, across, recv):
    tall, wide = grid_of(count)
    dst = pieces[c][1]
    for other in across:
        for i in range(tall):
            shard = ((row + i) % tall) * wide + other % wide
            sends.arrived(dst(shard), recv.at[shard, c], {"dp": other})


def halves(src, full, depth):
    half = depth // 2
    return [
        (src.at[pl.ds(i * half, half)], lambda j, i=i: full.at[j, pl.ds(i * half, half)])
        for i in range(2)
    ]


def weights_kernel(count, in_ref, out_ref, full_in, full_out, send, recv, own):
    me, row, across, along = neighbours(count)
    depth = in_ref.shape[0]
    meet([{"dp": j} for j in along + across])
    pieces = halves(in_ref, full_in, depth) + halves(out_ref, full_out, depth)
    sends = Sends(send)
    spread(sends, pieces, me, across, along, recv)
    mine = [
        pltpu.make_async_copy(in_ref, full_in.at[me], own.at[0]),
        pltpu.make_async_copy(out_ref, full_out.at[me], own.at[1]),
    ]
    for copy in mine:
        copy.start()
    for c in range(len(pieces)):
        relay(sends, pieces, c, across, along, recv)
    for c in range(len(pieces)):
        collect(sends, pieces, c, row, count, across, recv)
    for copy in mine:
        copy.wait()
    sends.finish()


def grads_kernel(
    count, cols_a, cols_b, acts_a, acts_b, small_ref, full, sliced, smalls, send, recv, own
):
    me, row, across, along = neighbours(count)
    core = lax.axis_index("tensor")
    depth = sliced.shape[-1]
    everyone = [{"dp": (me + i) % count} for i in range(1, count)]
    crossed = [{"dp": (me + i) % count, "tensor": 1 - core} for i in range(count)]
    meet(everyone + crossed)
    pieces = [(cols_a, lambda j: full.at[j, 0]), (cols_b, lambda j: full.at[j, 1])]
    acts = (acts_a, acts_b)
    sends = Sends(send)
    spread(sends, pieces, me, across, along, recv)
    for peer in everyone:
        block = pl.ds(pl.multiple_of(peer["dp"] * depth, depth), depth)
        for i in range(2):
            sends.start(acts[i].at[:, :, block], sliced.at[me, i], recv.at[me, 5 + i], peer)
    for peer in everyone + crossed:
        sends.start(small_ref, smalls.at[core, me], recv.at[me, 3 + core], peer)
    block = pl.ds(pl.multiple_of(me * depth, depth), depth)
    mine = [
        pltpu.make_async_copy(cols_a, full.at[me, 0], own.at[0]),
        pltpu.make_async_copy(cols_b, full.at[me, 1], own.at[1]),
        pltpu.make_async_copy(acts_a.at[:, :, block], sliced.at[me, 0], own.at[3]),
        pltpu.make_async_copy(acts_b.at[:, :, block], sliced.at[me, 1], own.at[4]),
        pltpu.make_async_copy(small_ref, smalls.at[core, me], own.at[2]),
    ]
    for copy in mine:
        copy.start()
    for c in range(2):
        relay(sends, pieces, c, across, along, recv)
    for c in range(2):
        collect(sends, pieces, c, row, count, across, recv)
    for peer in everyone:
        j = peer["dp"]
        for i in range(2):
            sends.arrived(sliced.at[j, i], recv.at[j, 5 + i], peer)
        sends.arrived(smalls.at[core, j], recv.at[j, 3 + core], peer)
    for peer in crossed:
        j = peer["dp"]
        sends.arrived(smalls.at[1 - core, j], recv.at[j, 4 - core], peer)
    for copy in mine:
        copy.wait()
    sends.finish()


ANY = pl.BlockSpec(memory_space=pl.ANY)


def gather_weights(w_in, w_out):
    count = lax.axis_size("dp")
    tall, wide = grid_of(count)
    sent = 4 * (tall + wide - 2 + (tall - 1) * (wide - 1))
    return pl.pallas_call(
        functools.partial(weights_kernel, count),
        out_shape=[jax.ShapeDtypeStruct((count,) + w.shape, w.dtype) for w in (w_in, w_out)],
        in_specs=[ANY] * 2,
        out_specs=[ANY] * 2,
        scratch_shapes=[
            pltpu.SemaphoreType.DMA((sent,)),
            pltpu.SemaphoreType.DMA((count, 4)),
            pltpu.SemaphoreType.DMA((2,)),
        ],
        compiler_params=pltpu.CompilerParams(collective_id=0, has_side_effects=True),
    )(w_in, w_out)


def exchange_grads(cols, cols_b, acts, acts_b, small):
    count = lax.axis_size("dp")
    tall, wide = grid_of(count)
    rows, width = acts.shape[1:]
    sent = 2 * (tall + wide - 2 + (tall - 1) * (wide - 1)) + 4 * count - 3
    return pl.pallas_call(
        functools.partial(grads_kernel, count),
        out_shape=[
            jax.ShapeDtypeStruct((count, 2) + cols.shape, cols.dtype),
            jax.ShapeDtypeStruct((count, 2, 2, rows, width // count), acts.dtype),
            jax.ShapeDtypeStruct((2, count) + small.shape, small.dtype),
        ],
        in_specs=[ANY] * 5,
        out_specs=[ANY] * 3,
        scratch_shapes=[
            pltpu.SemaphoreType.DMA((sent,)),
            pltpu.SemaphoreType.DMA((count, 7)),
            pltpu.SemaphoreType.DMA((5,)),
        ],
        compiler_params=pltpu.CompilerParams(collective_id=1, has_side_effects=True),
    )(cols, cols_b, acts, acts_b, small)


def rope_tables(length, width):
    half_width = width // 2
    freqs = jnp.exp(jnp.arange(half_width, dtype=jnp.float32) * (-2.0 * math.log(THETA) / width))
    angles = jnp.arange(length, dtype=jnp.float32)[:, None] * freqs[None, :]
    return (jnp.cos(angles), jnp.sin(angles))


def nt(left, right):
    return lax.dot_general(
        left, right, (((1,), (1,)), ((), ())), preferred_element_type=jnp.float32
    )


def tn(left, right):
    return lax.dot_general(
        left, right, (((0,), (0,)), ((), ())), preferred_element_type=jnp.float32
    )


def nn(left, right):
    return jnp.dot(left, right, preferred_element_type=jnp.float32)


def turn(vectors, tables, sign):
    cos_tab = tables[0, : vectors.shape[0]]
    sin_tab = tables[1, : vectors.shape[0]]
    return vectors * cos_tab + pltpu.roll(vectors, HD // 2, 1) * (sign * sin_tab)


def head_norm(raw_heads):
    inverse = lax.rsqrt(jnp.mean(raw_heads * raw_heads, axis=-1, keepdims=True) + EPSILON)
    return (raw_heads * inverse, inverse)


def unit_back(grad_unit, unit_row_vectors, inverse):
    return inverse * (
        grad_unit
        - unit_row_vectors * jnp.mean(grad_unit * unit_row_vectors, axis=-1, keepdims=True)
    )


def tall_heads(wide):
    return jnp.concatenate(
        [wide[:, h * HD : (h + 1) * HD] for h in range(wide.shape[1] // HD)], axis=0
    )


def wide_heads(tall, rows):
    return jnp.concatenate(
        [tall[h * rows : (h + 1) * rows] for h in range(tall.shape[0] // rows)], axis=1
    )


def lower(tall, rows):
    return jnp.concatenate(
        [tall[h + rows : h + 2 * rows] for h in range(0, tall.shape[0], 2 * rows)], axis=0
    )


def slot_kernel(
    xf_ref, xb_ref, g_ref, gain_ref, qk_ref, tables, wi_ref, wo_ref,
    parts_ref, cols_ref, acts_ref, terms_ref,
):
    rows = xf_ref.shape[0]
    q_width = wo_ref.shape[1]
    scale = 1.0 / math.sqrt(HD)
    q_gain, k_gain = qk_ref[0:1], qk_ref[1:2]
    x = jnp.concatenate([xf_ref[...], xb_ref[...]], axis=0).astype(jnp.float32)
    unit, _ = head_norm(x)
    normed = (unit * gain_ref[...]).astype(jnp.bfloat16)
    acts_ref[0] = normed[rows:]
    acts_ref[1] = g_ref[...]
    qkv = nn(normed, wi_ref[...])
    q_unit, q_inv = head_norm(tall_heads(qkv[:, :q_width]))
    k_unit, k_inv = head_norm(qkv[:, q_width : q_width + HD])
    values = qkv[:, q_width + HD :].astype(jnp.bfloat16)
    queries = turn(q_unit * q_gain, tables, 1.0).astype(jnp.bfloat16)
    keys = turn(k_unit * k_gain, tables, 1.0).astype(jnp.bfloat16)
    scores = nt(queries, keys) * scale
    row = lax.rem(lax.broadcasted_iota(jnp.int32, scores.shape, 0), 2 * rows)
    col = lax.broadcasted_iota(jnp.int32, scores.shape, 1)
    seen = (row >= col) & ((row < rows) | (col >= rows))
    expd = jnp.where(seen, jnp.exp(scores), 0.0)
    probs = expd / jnp.sum(expd, axis=-1, keepdims=True)
    probs_b = probs.astype(jnp.bfloat16)
    attended = wide_heads(nn(probs_b, values), 2 * rows).astype(jnp.bfloat16)
    parts_ref[:rows] = nt(attended[:rows], wo_ref[...]).astype(jnp.bfloat16)
    d_attn = tall_heads(nn(g_ref[...], wo_ref[...])).astype(jnp.bfloat16)
    probs, q_unit, q_inv = lower(probs, rows), lower(q_unit, rows), lower(q_inv, rows)
    probs_b, queries = lower(probs_b, rows), lower(queries, rows)
    d_probs = nt(d_attn, values)
    d_scores = probs * (d_probs - jnp.sum(probs * d_probs, axis=-1, keepdims=True)) * scale
    d_scores = d_scores.astype(jnp.bfloat16)
    d_value = tn(probs_b, d_attn)[rows:].astype(jnp.bfloat16)
    d_query = turn(nn(d_scores, keys), tables, -1.0)
    d_key = turn(tn(d_scores, queries)[rows:], tables, -1.0)
    k_unit, k_inv = k_unit[rows:], k_inv[rows:]
    terms_ref[0:1] = jnp.sum(d_query * q_unit, axis=0, keepdims=True)
    terms_ref[1:2] = jnp.sum(d_key * k_unit, axis=0, keepdims=True)
    q_grad = wide_heads(unit_back(d_query * q_gain, q_unit, q_inv), rows).astype(jnp.bfloat16)
    k_grad = unit_back(d_key * k_gain, k_unit, k_inv).astype(jnp.bfloat16)
    columns = jnp.concatenate([q_grad, k_grad, d_value], axis=1)
    cols_ref[:, : columns.shape[1]] = columns
    cols_ref[:, columns.shape[1] :] = attended[rows:]
    parts_ref[rows:] = nt(columns, wi_ref[...]).astype(jnp.bfloat16)


def finish_kernel(xf_ref, xb_ref, g_ref, gain_ref, mine_ref, other_ref, out_ref, back_ref, term_ref):
    rows = xf_ref.shape[0]
    total = mine_ref[...].astype(jnp.float32) + other_ref[...].astype(jnp.float32)
    out_ref[...] = (xf_ref[...].astype(jnp.float32) + total[:rows]).astype(jnp.bfloat16)
    unit, inverse = head_norm(xb_ref[...].astype(jnp.float32))
    d_normed = total[rows:]
    d_input = g_ref[...].astype(jnp.float32) + unit_back(d_normed * gain_ref[...], unit, inverse)
    back_ref[...] = d_input.astype(jnp.bfloat16)
    term_ref[...] = jnp.sum(d_normed * unit, axis=0, keepdims=True)


ROOM = pltpu.CompilerParams(vmem_limit_bytes=48 * 1024 * 1024)


def run_slot(x_forward, x_backward, cot_rows, norm_scale, weights, qk_gains, tables):
    rows, width = x_forward.shape
    w_in, w_out = weights
    shape = jax.ShapeDtypeStruct
    parts, cols, acts, terms = pl.pallas_call(
        slot_kernel,
        out_shape=[
            shape((2 * rows, width), jnp.bfloat16),
            shape((rows, w_in.shape[1] + w_out.shape[1]), jnp.bfloat16),
            shape((2, rows, width), jnp.bfloat16),
            shape((2, HD), jnp.float32),
        ],
        compiler_params=ROOM,
    )(x_forward, x_backward, cot_rows, norm_scale, qk_gains, tables, w_in, w_out)
    other = lax.ppermute(parts, "tensor", [(0, 1), (1, 0)])
    layer_out, d_input, norm_term = pl.pallas_call(
        finish_kernel,
        out_shape=[
            shape((rows, width), jnp.bfloat16),
            shape((rows, width), jnp.bfloat16),
            shape((1, width), jnp.float32),
        ],
        compiler_params=ROOM,
    )(x_forward, x_backward, cot_rows, norm_scale, parts, other)
    return layer_out, d_input, cols, acts, norm_term, terms


def local(
    fwd_input,
    fresh_input,
    cotangent,
    fresh_cotangent,
    stash,
    norm_gain,
    qk_gain,
    w_query,
    w_key,
    w_value,
    w_out,
):
    q_width = w_query.shape[2]
    k_width = w_key.shape[2]
    left_width = q_width + 2 * k_width
    full_in, full_o = gather_weights(
        jnp.concatenate([w_query[0], w_key[0], w_value[0]], axis=1), w_out[0]
    )
    full_in = full_in.reshape(-1, left_width)
    full_o = full_o.reshape(-1, w_out.shape[2])
    weights = (full_in, full_o)
    norm_scale = norm_gain
    qk_gains = qk_gain[0]
    row_count = fwd_input.shape[1]
    cos_tab, sin_tab = rope_tables(row_count, HD)
    tables = jnp.stack(
        [
            jnp.concatenate([cos_tab, cos_tab], axis=1),
            jnp.concatenate([-sin_tab, sin_tab], axis=1),
        ]
    )
    tables = jnp.tile(tables, (1, 2 * q_width // HD, 1))
    section_position_index = lax.axis_index("section")
    section_total = lax.axis_size("section")
    bit_order = list(range(section_total.bit_length() - 1))
    reloaded = stash[0]
    for bit_index in bit_order:
        reloaded = swapped(reloaded, "section", bit_index)
    first_slot = run_slot(
        fwd_input[0], reloaded[0], cotangent[0], norm_scale, weights, qk_gains, tables
    )
    arrived = passed_along(first_slot[0], "section", 1)
    second_input = jnp.where(section_position_index == 0, fresh_input, arrived)
    returned = passed_along(first_slot[1], "section", -1)
    second_cot = jnp.where(section_position_index == section_total - 1, fresh_cotangent, returned)
    second_slot = run_slot(
        second_input, reloaded[1], second_cot, norm_scale, weights, qk_gains, tables
    )
    out_activations = jnp.stack([first_slot[0], second_slot[0]])[None]
    grad_input = jnp.stack([first_slot[1], second_slot[1]])[None]
    grad_scale = 1.0 / math.sqrt(2 * row_count * lax.axis_size("dp"))
    contract = (((0,), (0,)), ((), ()))
    norm_term = first_slot[4] + second_slot[4]
    qk_term = first_slot[5] + second_slot[5]
    feature_rows = norm_term.shape[1] // HD
    small = jnp.concatenate(
        [norm_term.reshape(feature_rows, HD), qk_term, jnp.zeros((6, HD), jnp.float32)], axis=0
    )
    gathered, sliced, smalls = exchange_grads(
        first_slot[2], second_slot[2], first_slot[3], second_slot[3], small * grad_scale
    )
    gathered = gathered.reshape(-1, gathered.shape[-1])
    sliced = jnp.moveaxis(sliced, 2, 0).reshape(2, -1, sliced.shape[-1])
    norm_total = jnp.sum(smalls[0, :, :feature_rows], axis=0).reshape(-1)
    qk_total = jnp.sum(smalls[:, :, feature_rows : feature_rows + 2], axis=(0, 1))
    left_term = lax.dot_general(
        sliced[0], gathered[:, :left_width], contract, preferred_element_type=jnp.float32
    )
    right_term = lax.dot_general(
        sliced[1], gathered[:, left_width:], contract, preferred_element_type=jnp.float32
    )
    left_term = left_term * grad_scale
    right_term = right_term * grad_scale
    grad_query = left_term[:, :q_width][None]
    grad_key = left_term[:, q_width : q_width + k_width][None]
    grad_value = left_term[:, q_width + k_width :][None]
    grad_out = right_term[None]
    return (
        out_activations,
        grad_input,
        grad_query,
        grad_key,
        grad_value,
        grad_out,
        norm_total[None],
        qk_total[None],
    )


def solution(mesh):
    return jax.shard_map(
        local,
        mesh=mesh,
        in_specs=(
            P("section", "dp", None),
            P("dp", None),
            P("section", "dp", None),
            P("dp", None),
            P("section", None, "dp", None),
            P("section", None),
            P("section", None, None),
            P("section", "dp", "tensor"),
            P("section", "dp", "tensor"),
            P("section", "dp", "tensor"),
            P("section", "dp", "tensor"),
        ),
        out_specs=(
            P("section", None, "dp", None),
            P("section", None, "dp", None),
            P("section", "dp", "tensor"),
            P("section", "dp", "tensor"),
            P("section", "dp", "tensor"),
            P("section", "dp", "tensor"),
            P("section", None),
            P("section", None, None),
        ),
        check_vma=False,
    )
```

time: 279 us -> 243 us (0.87)
  matrix products: 46.9 us -> 4.51 us
  Pallas kernels: 191 us -> 208 us
  local copies, waits for them, and re-layouts: 14.8 us -> 7.49 us
  other arithmetic: 13.2 us -> 7.23 us
  waiting for transfers between devices: 5.04 us -> 8.79 us
    dot_general x36 -> x0, matrix products: 42.4 us -> none  [the longest x4 9.75 us: attend_local(): jnp.dot(normed, w_q, preferred_element_type=jnp.float32)]
    pallas_call x0 -> x4, Pallas kernels: none -> 16.7 us  [the longest x2 16 us: run_slot(): pl.pallas_call(slot_kernel, out_shape=[shape((2 * rows, width), jnp.bfloa...]
    dot_general x2 -> x0, local copies, waits for them, and re-layouts: 11.2 us -> none  [attend_local(): jnp.dot(normed, w_q, preferred_element_type=jnp.float32)]
    unnamed x27 -> x24, local copies, waits for them, and re-layouts: 0.14 us -> 4.45 us
  transfers between devices with their start and end apart: 5 -> 5, of which waited for: 2 -> 4; matrix products, arithmetic and copies ran while one was open for 9% -> 1% of each run, Pallas kernels for 50% -> 58%
where the time goes in v3:
time: 243 us
  Pallas kernels  208 us (86%)
  waiting for transfers between devices  8.79 us (4%)
  local copies, waits for them, and re-layouts  7.49 us (3%)
  other arithmetic  7.23 us (3%)
  starting transfers between devices  5.44 us (2%)
  matrix products  4.51 us (2%)
    pallas_call x1, Pallas kernels, gather_weights(): pl.pallas_call(functools.partial(weights_kernel, count), out_shape=[jax.S...  140 us
    pallas_call x1, Pallas kernels, exchange_grads(): pl.pallas_call(functools.partial(grads_kernel, count), out_shape=[jax.Sha...  51.2 us
    pallas_call x2, Pallas kernels, run_slot(): pl.pallas_call(slot_kernel, out_shape=[shape((2 * rows, width), jnp.bfloa...  16 us
    ppermute x2, waiting for transfers between devices, passed_along(): return lax.ppermute(array, axis, pairs)  5.83 us
  transfers between devices with their start and end apart: 5, of which 4 were waited for; matrix products, arithmetic and copies ran while one was open for 1% of the time, Pallas kernels for 58%

profile of v3, /device:TPU:12, one launch (start us, length us, event | category | flops | bytes accessed | tf_op | source)
XLA Modules:
  0.0 242.6 jit_solution(1478075439193384914)
XLA Ops:
  0.6 0.6 collective-permute-start
  1.2 2.0 pad_maximum_fusion.in_ref
  3.2 0.1 fusion.4
  3.3 140.4 %shard_map.170 = (bf16[8,256,1280]{2,1,0:T(8,128)(2,1)}, bf16[8,256,1024]{2,1,0:T(8,128)(2,1)}) custom-call(bf16[256,1280]{1,0:T(8,128)(2,1)} %pad_maximum_fusion.in_ref, bf16[256,1024]{1,0:T(8,128)(2,1)} %bitcast.65), custom_call_target="tpu_custom_call" | custom-call | tf_op jit(solution)/shard_map/pallas_call | solution.py:187
  143.8 0.1 maximum_bitcast_fusion.2
  143.8 0.0 collective-permute-done
  143.9 0.1 tile.4
  143.9 0.0 copy-done.2
  143.9 0.0 copy-done.3
  144.0 0.0 copy-done.8
  144.0 0.0 copy-done.9
  144.0 0.0 copy-start
  144.0 2.2 copy-done
  146.2 8.0 %shard_map.171 = (bf16[64,2048]{1,0:T(8,128)(2,1)S(1)}, bf16[32,2304]{1,0:T(8,128)(2,1)S(1)}, bf16[2,32,2048]{2,1,0:T(8,128)(2,1)S(1)}, f32[2,128]{1,0:T(2,128)S(1)}) custom-call(bf16[32,2048]{1,0:T(8,128)(2,1)S(1)} %bitcast.48, bf16[32,2048]{1,0:T(8,128)(2,1)S(1)} %get-tuple-element.51.xb_ref, bf16[32,2048]{1,0:T(8,128)(2,1)S(1)} %bitcast.50, ...), custom_call_target="tpu_custom_call" | custom-call | tf_op jit(solution)/shard_map/pallas_call | solution.py:349
  154.2 0.0 copy-start.4
  154.2 0.0 copy-start.6
  154.2 0.0 copy-start.11
  154.3 0.1 collective-permute-start.1
  154.3 1.5 collective-permute-done.1.other_ref
  155.9 0.3 shard_map.172
  156.2 0.0 copy-done.4
  156.2 0.0 copy-done.6
  156.2 3.4 %collective-permute-start.3 = (bf16[32,2048]{1,0:T(8,128)(2,1)S(1)}, bf16[32,2048]{1,0:T(8,128)(2,1)S(1)}, u32[]{:S(2)}, u32[]{:S(2)}) collective-permute-start(bf16[32,2048]{1,0:T(8,128)(2,1)S(1)} %get-tuple-element.31), channel_id=1, source_target_pairs={{16,0},{17,1},{18,2},{19,3},{20,4},{21,5},{22,6},{23,7},{24,8},{25... | collective-permute-start | bytes 393224 | tf_op jit(solution)/shard_map/ppermute | solution.py:31
  159.6 1.3 collective-permute-start.2
  160.9 1.7 collective-permute-done.3
  162.7 0.0 copy-done.10
  162.7 4.1 %collective-permute-done.2 = bf16[32,2048]{1,0:T(8,128)(2,1)S(1)} collective-permute-done((bf16[32,2048]{1,0:T(8,128)(2,1)S(1)}, bf16[32,2048]{1,0:T(8,128)(2,1)S(1)}, u32[]{:S(2)}, u32[]{:S(2)}) %collective-permute-start.2) | collective-permute-done | bytes 131104 | tf_op jit(solution)/shard_map/ppermute | solution.py:31
  166.8 0.0 copy-done.11
  166.8 0.0 copy-start.1
  166.8 2.2 copy-done.1
  169.0 8.0 %shard_map.173 = (bf16[64,2048]{1,0:T(8,128)(2,1)S(1)}, bf16[32,2304]{1,0:T(8,128)(2,1)S(1)}, bf16[2,32,2048]{2,1,0:T(8,128)(2,1)S(1)}, f32[2,128]{1,0:T(2,128)S(1)}) custom-call(bf16[32,2048]{1,0:T(8,128)(2,1)S(1)} %broadcast_select_fusion.1.xf_ref, bf16[32,2048]{1,0:T(8,128)(2,1)S(1)} %get-tuple-element.50.xb_ref, ...), custom_call_target="tpu_custom_call" | custom-call | tf_op jit(solution)/shard_map/pallas_call | solution.py:349
  177.0 0.0 copy-start.5
  177.0 0.0 copy-start.7
  177.1 0.1 collective-permute-start.4
  177.1 0.1 pad.2.clone
  177.2 1.4 collective-permute-done.4.other_ref
  178.7 0.3 shard_map.174
  179.0 0.7 maximum_multiply_fusion.small_ref
  179.7 51.2 %shard_map.175 = (bf16[8,2,32,2304]{3,2,1,0:T(8,128)(2,1)}, bf16[8,2,2,32,256]{4,3,2,1,0:T(8,128)(2,1)}, f32[2,8,24,128]{3,2,1,0:T(8,128)}) custom-call(bf16[32,2304]{1,0:T(8,128)(2,1)} %copy-done.6, bf16[32,2304]{1,0:T(8,128)(2,1)} %copy-done.7, bf16[2,32,2048]{2,1,0:T(8,128)(2,1)} %copy-done.4, bf16[2,32,2048]{2,1,0:T(8,128)(2,1)} %copy-done.5, ...), custom_call_target="tpu_custom_call" | custom-call | tf_op jit(solution)/shard_map/pallas_call | solution.py:206
  230.9 1.1 fusion.6
  232.0 1.8 convolution_multiply_fusion
  233.8 1.1 slice_bitcast_fusion
  234.9 0.7 slice_bitcast_fusion.1
  235.7 1.4 slice_reduce_fusion
  237.1 1.4 slice_reduce_fusion.1
  238.5 2.7 %fusion = f32[1,256,1024]{2,1,0:T(8,128)} fusion(bf16[512,256]{1,0:T(8,128)(2,1)S(1)} %bitcast.62, bf16[512,2304]{1,0:T(8,128)(2,1)} %bitcast.61), kind=kOutput, calls=%fused_computation.2 | convolution fusion | flops 268697600 | bytes 2359296 | tf_op jit(solution)/shard_map/dot_general | solution.py:441
  241.2 0.7 maximum_bitcast_fusion.1
  241.9 0.7 maximum_bitcast_fusion
  (15 shorter events, 0.1 us)
Async XLA Ops:
  0.6 143.2 %collective-permute-start = (bf16[2,32,2048]{2,1,0:T(8,128)(2,1)}, bf16[2,32,2048]{2,1,0:T(8,128)(2,1)S(1)}, u32[]{:S(2)}, u32[]{:S(2)}) collective-permute-start(bf16[2,32,2048]{2,1,0:T(8,128)(2,1)} %bitcast.72), channel_id=1, source_target_pairs={{0,16},{16,0},{1,17},{17,1},{2,18},{18,2},{3,19},{19,3},{4,20},{20... | collective-permute-start | bytes 786440 | tf_op jit(solution)/shard_map/ppermute | solution.py:25
  3.2 140.7 %copy-start.2 = (bf16[1,32,2048]{2,1,0:T(8,128)(2,1)S(1)}, bf16[1,32,2048]{2,1,0:T(8,128)(2,1)}, u32[]{:S(2)}) copy-start(bf16[1,32,2048]{2,1,0:T(8,128)(2,1)} %param.11) | copy-start | bytes 393220
  3.2 140.7 %copy-start.3 = (bf16[1,32,2048]{2,1,0:T(8,128)(2,1)S(1)}, bf16[1,32,2048]{2,1,0:T(8,128)(2,1)}, u32[]{:S(2)}) copy-start(bf16[1,32,2048]{2,1,0:T(8,128)(2,1)} %param.13) | copy-start | bytes 393220
  3.2 140.7 %copy-start.8 = (f32[1,2048]{1,0:T(1,128)S(1)}, f32[1,2048]{1,0:T(1,128)}, u32[]{:S(2)}) copy-start(f32[1,2048]{1,0:T(1,128)} %gain_ref.7) | copy-start | bytes 24580
  3.2 140.7 %copy-start.9 = (f32[1,2,128]{2,1,0:T(2,128)S(1)}, f32[1,2,128]{2,1,0:T(2,128)}, u32[]{:S(2)}) copy-start(f32[1,2,128]{2,1,0:T(2,128)} %param.17) | copy-start | bytes 3076
  144.0 2.2 copy-start
  146.2 16.5 %copy-start.10 = (bf16[32,2048]{1,0:T(8,128)(2,1)S(1)}, bf16[32,2048]{1,0:T(8,128)(2,1)}, u32[]{:S(2)}) copy-start(bf16[32,2048]{1,0:T(8,128)(2,1)} %param.14) | copy-start | bytes 393220
  154.2 2.0 copy-start.4
  154.2 1.9 copy-start.6
  154.2 12.6 %copy-start.11 = (bf16[32,2048]{1,0:T(8,128)(2,1)S(1)}, bf16[32,2048]{1,0:T(8,128)(2,1)}, u32[]{:S(2)}) copy-start(bf16[32,2048]{1,0:T(8,128)(2,1)} %param.12) | copy-start | bytes 393220
  154.3 1.6 collective-permute-start.1
  156.2 6.5 %collective-permute-start.3 = (bf16[32,2048]{1,0:T(8,128)(2,1)S(1)}, bf16[32,2048]{1,0:T(8,128)(2,1)S(1)}, u32[]{:S(2)}, u32[]{:S(2)}) collective-permute-start(bf16[32,2048]{1,0:T(8,128)(2,1)S(1)} %get-tuple-element.31), channel_id=1, source_target_pairs={{16,0},{17,1},{18,2},{19,3},{20,4},{21,5},{22,6},{23,7},{24,8},{25... | collective-permute-start | bytes 393224 | tf_op jit(solution)/shard_map/ppermute | solution.py:31
  159.6 7.2 %collective-permute-start.2 = (bf16[32,2048]{1,0:T(8,128)(2,1)S(1)}, bf16[32,2048]{1,0:T(8,128)(2,1)S(1)}, u32[]{:S(2)}, u32[]{:S(2)}) collective-permute-start(bf16[32,2048]{1,0:T(8,128)(2,1)S(1)} %get-tuple-element.30), channel_id=1, source_target_pairs={{0,16},{1,17},{2,18},{3,19},{4,20},{5,21},{6,22},{7,23},{8,24},{9,... | collective-permute-start | bytes 393224 | tf_op jit(solution)/shard_map/ppermute | solution.py:31
  166.8 2.2 copy-start.1
  177.0 2.0 copy-start.5
  177.0 1.9 copy-start.7
  177.1 1.6 collective-permute-start.4

commit v4 on v3

--- a/solution.py
+++ b/solution.py
@@ -48,7 +48,7 @@
         self.sems = sems
         self.started = []
 
-    def start(self, src, dst, recv, peer):
+    def start(self, src, dst, recv, peer, cond=None):
         copy = pltpu.make_async_remote_copy(
             src_ref=src,
             dst_ref=dst,
@@ -56,8 +56,11 @@
             recv_sem=recv,
             device_id=peer,
         )
-        copy.start()
-        self.started.append(copy)
+        if cond is None:
+            copy.start()
+        else:
+            pl.when(cond)(copy.start)
+        self.started.append((cond, copy))
 
     def arrived(self, dst, recv, peer):
         pltpu.make_async_remote_copy(
@@ -65,8 +68,18 @@
         ).wait_recv()
 
     def finish(self):
-        for copy in self.started:
-            copy.wait_send()
+        for cond, copy in self.started:
+            if cond is None:
+                copy.wait_send()
+            else:
+                pl.when(cond)(copy.wait_send)
+
+
+def relayed(count, pieces, early):
+    tall, wide = grid_of(count)
+    plain = wide + 1 + (tall - 1) * 2 * wide
+    first = wide + 1 + 2 * (wide - 1) + (tall - 1) * 2 * wide
+    return (pieces - early) * plain + early * first
 
 
 def neighbours(count):
@@ -78,54 +91,93 @@
     return me, row, across, along
 
 
-def spread(sends, pieces, me, across, along, recv):
-    for c, (src, dst) in enumerate(pieces):
-        for peer in along + across:
-            sends.start(src, dst(me), recv.at[me, c], {"dp": peer})
-
-
-def relay(sends, pieces, c, across, along, recv):
-    dst = pieces[c][1]
-    for peer in along:
-        sends.arrived(dst(peer), recv.at[peer, c], {"dp": peer})
-        for other in across:
-            sends.start(dst(peer), dst(peer), recv.at[peer, c], {"dp": other})
-
-
-def collect(sends, pieces, c, row, count, across, recv):
-    tall, wide = grid_of(count)
-    dst = pieces[c][1]
-    for other in across:
-        for i in range(tall):
-            shard = ((row + i) % tall) * wide + other % wide
-            sends.arrived(dst(shard), recv.at[shard, c], {"dp": other})
-
-
-def halves(src, full, depth):
-    half = depth // 2
+def cut(src, full, depth, parts):
+    part = depth // parts
     return [
-        (src.at[pl.ds(i * half, half)], lambda j, i=i: full.at[j, pl.ds(i * half, half)])
-        for i in range(2)
+        (src.at[pl.ds(i * part, part)], lambda j, i=i: full.at[j, pl.ds(i * part, part)])
+        for i in range(parts)
     ]
+
+
+class Relay:
+    def __init__(self, count, pieces, early, sends, recv):
+        self.tall, self.wide = grid_of(count)
+        self.me, self.row, self.across, self.along = neighbours(count)
+        self.pieces, self.early, self.sends, self.recv = pieces, early, sends, recv
+        self.up, self.down = self.row < self.tall - 1, self.row > 0
+
+    def pass_on(self, cond, c, shard, peer, own=False):
+        src, dst = self.pieces[c]
+        src = src if own else dst(shard)
+        self.sends.start(src, dst(shard), self.recv.at[shard, c], {"dp": peer}, cond)
+
+    def begin(self, chosen):
+        for c in chosen:
+            for peer in self.across:
+                self.pass_on(None, c, self.me, peer, True)
+            self.pass_on(self.up, c, self.me, self.me + self.wide, True)
+            self.pass_on(self.down, c, self.me, self.me - self.wide, True)
+
+    def take(self, cond, c, shard):
+        arrive = functools.partial(
+            self.sends.arrived, self.pieces[c][1](shard), self.recv.at[shard, c], {"dp": self.me}
+        )
+        if cond is None:
+            arrive()
+        else:
+            pl.when(cond)(arrive)
+
+    def hop(self, c, d):
+        wide, me = self.wide, self.me
+        shifts = [0] + [p - me for p in self.across] if c in self.early else [0]
+        if d == 1:
+            for shift in shifts[1:]:
+                self.take(None, c, me + shift)
+                self.pass_on(self.up, c, me + shift, me + wide)
+                self.pass_on(self.down, c, me + shift, me - wide)
+        for shift in shifts:
+            for near, here, on, after in (
+                (me - d * wide, self.row >= d, self.up, me + wide),
+                (me + d * wide, self.row + d < self.tall, self.down, me - wide),
+            ):
+                self.take(here, c, near + shift)
+                self.pass_on(here & on, c, near + shift, after)
+                if c not in self.early:
+                    for peer in self.across:
+                        self.pass_on(here, c, near, peer)
+
+    def run(self, chosen):
+        for wave in range(len(chosen) + self.tall - 2):
+            for d in range(1, self.tall):
+                if 0 <= wave - d + 1 < len(chosen):
+                    self.hop(chosen[wave - d + 1], d)
+
+    def end(self, chosen):
+        for c in chosen:
+            if c in self.early:
+                continue
+            for other in self.across:
+                for i in range(self.tall):
+                    self.take(None, c, ((self.row + i) % self.tall) * self.wide + other % self.wide)
 
 
 def weights_kernel(count, in_ref, out_ref, full_in, full_out, send, recv, own):
     me, row, across, along = neighbours(count)
     depth = in_ref.shape[0]
     meet([{"dp": j} for j in along + across])
-    pieces = halves(in_ref, full_in, depth) + halves(out_ref, full_out, depth)
     sends = Sends(send)
-    spread(sends, pieces, me, across, along, recv)
+    pieces = cut(in_ref, full_in, depth, 4) + cut(out_ref, full_out, depth, 4)
+    relay = Relay(count, pieces, (0,), sends, recv)
+    order = list(range(8))
+    relay.begin(order)
     mine = [
         pltpu.make_async_copy(in_ref, full_in.at[me], own.at[0]),
         pltpu.make_async_copy(out_ref, full_out.at[me], own.at[1]),
     ]
     for copy in mine:
         copy.start()
-    for c in range(len(pieces)):
-        relay(sends, pieces, c, across, along, recv)
-    for c in range(len(pieces)):
-        collect(sends, pieces, c, row, count, across, recv)
+    relay.run(order)
+    relay.end(order)
     for copy in mine:
         copy.wait()
     sends.finish()
@@ -140,16 +192,22 @@
     everyone = [{"dp": (me + i) % count} for i in range(1, count)]
     crossed = [{"dp": (me + i) % count, "tensor": 1 - core} for i in range(count)]
     meet(everyone + crossed)
-    pieces = [(cols_a, lambda j: full.at[j, 0]), (cols_b, lambda j: full.at[j, 1])]
+    half = cols_a.shape[0] // 2
+    pieces = [
+        (cols.at[pl.ds(p * half, half)], lambda j, i=i, p=p: full.at[j, i, pl.ds(p * half, half)])
+        for i, cols in enumerate((cols_a, cols_b))
+        for p in range(2)
+    ]
     acts = (acts_a, acts_b)
     sends = Sends(send)
-    spread(sends, pieces, me, across, along, recv)
+    relay = Relay(count, pieces, (), sends, recv)
+    relay.begin(range(4))
     for peer in everyone:
         block = pl.ds(pl.multiple_of(peer["dp"] * depth, depth), depth)
         for i in range(2):
-            sends.start(acts[i].at[:, :, block], sliced.at[me, i], recv.at[me, 5 + i], peer)
+            sends.start(acts[i].at[:, :, block], sliced.at[me, i], recv.at[me, 6 + i], peer)
     for peer in everyone + crossed:
-        sends.start(small_ref, smalls.at[core, me], recv.at[me, 3 + core], peer)
+        sends.start(small_ref, smalls.at[core, me], recv.at[me, 4 + core], peer)
     block = pl.ds(pl.multiple_of(me * depth, depth), depth)
     mine = [
         pltpu.make_async_copy(cols_a, full.at[me, 0], own.at[0]),
@@ -160,18 +218,16 @@
     ]
     for copy in mine:
         copy.start()
-    for c in range(2):
-        relay(sends, pieces, c, across, along, recv)
-    for c in range(2):
-        collect(sends, pieces, c, row, count, across, recv)
+    relay.run(range(4))
+    relay.end(range(4))
     for peer in everyone:
         j = peer["dp"]
         for i in range(2):
-            sends.arrived(sliced.at[j, i], recv.at[j, 5 + i], peer)
-        sends.arrived(smalls.at[core, j], recv.at[j, 3 + core], peer)
+            sends.arrived(sliced.at[j, i], recv.at[j, 6 + i], peer)
+        sends.arrived(smalls.at[core, j], recv.at[j, 4 + core], peer)
     for peer in crossed:
         j = peer["dp"]
-        sends.arrived(smalls.at[1 - core, j], recv.at[j, 4 - core], peer)
+        sends.arrived(smalls.at[1 - core, j], recv.at[j, 5 - core], peer)
     for copy in mine:
         copy.wait()
     sends.finish()
@@ -182,8 +238,7 @@
 
 def gather_weights(w_in, w_out):
     count = lax.axis_size("dp")
-    tall, wide = grid_of(count)
-    sent = 4 * (tall + wide - 2 + (tall - 1) * (wide - 1))
+    sent = relayed(count, 8, 1)
     return pl.pallas_call(
         functools.partial(weights_kernel, count),
         out_shape=[jax.ShapeDtypeStruct((count,) + w.shape, w.dtype) for w in (w_in, w_out)],
@@ -191,7 +246,7 @@
         out_specs=[ANY] * 2,
         scratch_shapes=[
             pltpu.SemaphoreType.DMA((sent,)),
-            pltpu.SemaphoreType.DMA((count, 4)),
+            pltpu.SemaphoreType.DMA((count, 8)),
             pltpu.SemaphoreType.DMA((2,)),
         ],
         compiler_params=pltpu.CompilerParams(collective_id=0, has_side_effects=True),
@@ -200,9 +255,8 @@
 
 def exchange_grads(cols, cols_b, acts, acts_b, small):
     count = lax.axis_size("dp")
-    tall, wide = grid_of(count)
     rows, width = acts.shape[1:]
-    sent = 2 * (tall + wide - 2 + (tall - 1) * (wide - 1)) + 4 * count - 3
+    sent = relayed(count, 4, 0) + 4 * count - 3
     return pl.pallas_call(
         functools.partial(grads_kernel, count),
         out_shape=[
@@ -214,7 +268,7 @@
         out_specs=[ANY] * 3,
         scratch_shapes=[
             pltpu.SemaphoreType.DMA((sent,)),
-            pltpu.SemaphoreType.DMA((count, 7)),
+            pltpu.SemaphoreType.DMA((count, 8)),
             pltpu.SemaphoreType.DMA((5,)),
         ],
         compiler_params=pltpu.CompilerParams(collective_id=1, has_side_effects=True),

time: 243 us -> 208 us (0.86); the launches traced: 243 us -> 205 us
  Pallas kernels: 208 us -> 171 us
    pallas_call x1, Pallas kernels: 140 us -> 102 us  [gather_weights(): pl.pallas_call(functools.partial(weights_kernel, count), out_shape=[jax.S...]
  transfers between devices with their start and end apart: 5 -> 5, of which waited for: 4 -> 4; matrix products, arithmetic and copies ran while one was open for 1% -> 1% of each run, Pallas kernels for 58% -> 50%
where the time goes in v4:
time: 208 us; the launch traced here: 205 us
  Pallas kernels  171 us (82%)
  waiting for transfers between devices  8.61 us (4%)
  local copies, waits for them, and re-layouts  7.49 us (4%)
  other arithmetic  7.23 us (3%)
  starting transfers between devices  5.62 us (3%)
  matrix products  4.5 us (2%)
    pallas_call x1, Pallas kernels, gather_weights(): pl.pallas_call(functools.partial(weights_kernel, count), out_shape=[jax.S...  102 us
    pallas_call x1, Pallas kernels, exchange_grads(): pl.pallas_call(functools.partial(grads_kernel, count), out_shape=[jax.Sha...  52.1 us
    pallas_call x2, Pallas kernels, run_slot(): pl.pallas_call(slot_kernel, out_shape=[shape((2 * rows, width), jnp.bfloa...  16 us
    ppermute x2, waiting for transfers between devices, passed_along(): return lax.ppermute(array, axis, pairs)  5.65 us
    ppermute x2, starting transfers between devices, passed_along(): return lax.ppermute(array, axis, pairs)  4.9 us
    unnamed x24, local copies, waits for them, and re-layouts  4.45 us
  transfers between devices with their start and end apart: 5, of which 4 were waited for; matrix products, arithmetic and copies ran while one was open for 1% of the time, Pallas kernels for 50%

profile of v4, /device:TPU:12, one launch (start us, length us, event | category | flops | bytes accessed | tf_op | source)
XLA Modules:
  0.0 205.0 jit_solution(6235581394850294841)
XLA Ops:
  0.6 0.6 collective-permute-start
  1.2 2.0 pad_maximum_fusion.in_ref
  3.2 0.1 fusion.4
  3.3 101.8 %shard_map.170 = (bf16[8,256,1280]{2,1,0:T(8,128)(2,1)}, bf16[8,256,1024]{2,1,0:T(8,128)(2,1)}) custom-call(bf16[256,1280]{1,0:T(8,128)(2,1)} %pad_maximum_fusion.in_ref, bf16[256,1024]{1,0:T(8,128)(2,1)} %bitcast.65), custom_call_target="tpu_custom_call" | custom-call | tf_op jit(solution)/shard_map/pallas_call | solution.py:242
  105.2 0.1 maximum_bitcast_fusion.2
  105.3 0.0 collective-permute-done
  105.3 0.1 tile.4
  105.4 0.0 copy-done.2
  105.4 0.0 copy-done.3
  105.4 0.0 copy-done.8
  105.4 0.0 copy-done.9
  105.4 0.0 copy-start
  105.4 2.2 %copy-done = bf16[8,256,1024]{2,1,0:T(8,128)(2,1)S(1)} copy-done((bf16[8,256,1024]{2,1,0:T(8,128)(2,1)S(1)}, bf16[8,256,1024]{2,1,0:T(8,128)(2,1)}, u32[]{:S(2)}) %copy-start) | copy-done | bytes 4194328
  107.6 8.0 %shard_map.171 = (bf16[64,2048]{1,0:T(8,128)(2,1)S(1)}, bf16[32,2304]{1,0:T(8,128)(2,1)S(1)}, bf16[2,32,2048]{2,1,0:T(8,128)(2,1)S(1)}, f32[2,128]{1,0:T(2,128)S(1)}) custom-call(bf16[32,2048]{1,0:T(8,128)(2,1)S(1)} %bitcast.48, bf16[32,2048]{1,0:T(8,128)(2,1)S(1)} %get-tuple-element.51.xb_ref, bf16[32,2048]{1,0:T(8,128)(2,1)S(1)} %bitcast.50, ...), custom_call_target="tpu_custom_call" | custom-call | tf_op jit(solution)/shard_map/pallas_call | solution.py:403
  115.6 0.0 copy-start.4
  115.7 0.0 copy-start.6
  115.7 0.0 copy-start.11
  115.7 0.1 collective-permute-start.1
  115.8 1.5 collective-permute-done.1.other_ref
  117.3 0.3 shard_map.172
  117.6 0.0 copy-done.4
  117.6 0.0 copy-done.6
  117.6 3.4 %collective-permute-start.3 = (bf16[32,2048]{1,0:T(8,128)(2,1)S(1)}, bf16[32,2048]{1,0:T(8,128)(2,1)S(1)}, u32[]{:S(2)}, u32[]{:S(2)}) collective-permute-start(bf16[32,2048]{1,0:T(8,128)(2,1)S(1)} %get-tuple-element.31), channel_id=1, source_target_pairs={{16,0},{17,1},{18,2},{19,3},{20,4},{21,5},{22,6},{23,7},{24,8},{25... | collective-permute-start | bytes 393224 | tf_op jit(solution)/shard_map/ppermute | solution.py:31
  121.1 1.5 collective-permute-start.2
  122.5 1.5 collective-permute-done.3
  124.1 0.0 copy-done.10
  124.1 4.1 %collective-permute-done.2 = bf16[32,2048]{1,0:T(8,128)(2,1)S(1)} collective-permute-done((bf16[32,2048]{1,0:T(8,128)(2,1)S(1)}, bf16[32,2048]{1,0:T(8,128)(2,1)S(1)}, u32[]{:S(2)}, u32[]{:S(2)}) %collective-permute-start.2) | collective-permute-done | bytes 131104 | tf_op jit(solution)/shard_map/ppermute | solution.py:31
  128.2 0.0 copy-done.11
  128.2 0.0 copy-start.1
  128.2 2.2 %copy-done.1 = bf16[8,256,1024]{2,1,0:T(8,128)(2,1)S(1)} copy-done((bf16[8,256,1024]{2,1,0:T(8,128)(2,1)S(1)}, bf16[8,256,1024]{2,1,0:T(8,128)(2,1)}, u32[]{:S(2)}) %copy-start.1) | copy-done | bytes 4194328
  130.4 8.0 %shard_map.173 = (bf16[64,2048]{1,0:T(8,128)(2,1)S(1)}, bf16[32,2304]{1,0:T(8,128)(2,1)S(1)}, bf16[2,32,2048]{2,1,0:T(8,128)(2,1)S(1)}, f32[2,128]{1,0:T(2,128)S(1)}) custom-call(bf16[32,2048]{1,0:T(8,128)(2,1)S(1)} %broadcast_select_fusion.1.xf_ref, bf16[32,2048]{1,0:T(8,128)(2,1)S(1)} %get-tuple-element.50.xb_ref, ...), custom_call_target="tpu_custom_call" | custom-call | tf_op jit(solution)/shard_map/pallas_call | solution.py:403
  138.4 0.0 copy-start.5
  138.5 0.0 copy-start.7
  138.5 0.1 collective-permute-start.4
  138.6 0.1 pad.2.clone
  138.6 1.4 collective-permute-done.4.other_ref
  140.1 0.3 shard_map.174
  140.4 0.7 maximum_multiply_fusion.small_ref
  141.1 52.1 %shard_map.175 = (bf16[8,2,32,2304]{3,2,1,0:T(8,128)(2,1)}, bf16[8,2,2,32,256]{4,3,2,1,0:T(8,128)(2,1)}, f32[2,8,24,128]{3,2,1,0:T(8,128)}) custom-call(bf16[32,2304]{1,0:T(8,128)(2,1)} %copy-done.6, bf16[32,2304]{1,0:T(8,128)(2,1)} %copy-done.7, bf16[2,32,2048]{2,1,0:T(8,128)(2,1)} %copy-done.4, bf16[2,32,2048]{2,1,0:T(8,128)(2,1)} %copy-done.5, ...), custom_call_target="tpu_custom_call" | custom-call | tf_op jit(solution)/shard_map/pallas_call | solution.py:260
  193.2 1.1 fusion.6
  194.3 1.8 convolution_multiply_fusion
  196.2 1.1 slice_bitcast_fusion
  197.3 0.7 slice_bitcast_fusion.1
  198.0 1.4 slice_reduce_fusion
  199.4 1.4 slice_reduce_fusion.1
  200.8 2.7 %fusion = f32[1,256,1024]{2,1,0:T(8,128)} fusion(bf16[512,256]{1,0:T(8,128)(2,1)S(1)} %bitcast.62, bf16[512,2304]{1,0:T(8,128)(2,1)} %bitcast.61), kind=kOutput, calls=%fused_computation.2 | convolution fusion | flops 268697600 | bytes 2359296 | tf_op jit(solution)/shard_map/dot_general | solution.py:495
  203.5 0.7 maximum_bitcast_fusion.1
  204.2 0.7 maximum_bitcast_fusion
  (15 shorter events, 0.1 us)
Async XLA Ops:
  0.6 104.6 %collective-permute-start = (bf16[2,32,2048]{2,1,0:T(8,128)(2,1)}, bf16[2,32,2048]{2,1,0:T(8,128)(2,1)S(1)}, u32[]{:S(2)}, u32[]{:S(2)}) collective-permute-start(bf16[2,32,2048]{2,1,0:T(8,128)(2,1)} %bitcast.72), channel_id=1, source_target_pairs={{0,16},{16,0},{1,17},{17,1},{2,18},{18,2},{3,19},{19,3},{4,20},{20... | collective-permute-start | bytes 786440 | tf_op jit(solution)/shard_map/ppermute | solution.py:25
  3.2 102.1 %copy-start.2 = (bf16[1,32,2048]{2,1,0:T(8,128)(2,1)S(1)}, bf16[1,32,2048]{2,1,0:T(8,128)(2,1)}, u32[]{:S(2)}) copy-start(bf16[1,32,2048]{2,1,0:T(8,128)(2,1)} %param.11) | copy-start | bytes 393220
  3.2 102.2 %copy-start.3 = (bf16[1,32,2048]{2,1,0:T(8,128)(2,1)S(1)}, bf16[1,32,2048]{2,1,0:T(8,128)(2,1)}, u32[]{:S(2)}) copy-start(bf16[1,32,2048]{2,1,0:T(8,128)(2,1)} %param.13) | copy-start | bytes 393220
  3.2 102.2 %copy-start.8 = (f32[1,2048]{1,0:T(1,128)S(1)}, f32[1,2048]{1,0:T(1,128)}, u32[]{:S(2)}) copy-start(f32[1,2048]{1,0:T(1,128)} %gain_ref.7) | copy-start | bytes 24580
  3.2 102.2 %copy-start.9 = (f32[1,2,128]{2,1,0:T(2,128)S(1)}, f32[1,2,128]{2,1,0:T(2,128)}, u32[]{:S(2)}) copy-start(f32[1,2,128]{2,1,0:T(2,128)} %param.17) | copy-start | bytes 3076
  105.4 2.2 %copy-start = (bf16[8,256,1024]{2,1,0:T(8,128)(2,1)S(1)}, bf16[8,256,1024]{2,1,0:T(8,128)(2,1)}, u32[]{:S(2)}) copy-start(bf16[8,256,1024]{2,1,0:T(8,128)(2,1)} %get-tuple-element.28) | copy-start | bytes 12582916
  107.6 16.5 %copy-start.10 = (bf16[32,2048]{1,0:T(8,128)(2,1)S(1)}, bf16[32,2048]{1,0:T(8,128)(2,1)}, u32[]{:S(2)}) copy-start(bf16[32,2048]{1,0:T(8,128)(2,1)} %param.14) | copy-start | bytes 393220
  115.6 2.0 copy-start.4
  115.7 1.9 copy-start.6
  115.7 12.5 %copy-start.11 = (bf16[32,2048]{1,0:T(8,128)(2,1)S(1)}, bf16[32,2048]{1,0:T(8,128)(2,1)}, u32[]{:S(2)}) copy-start(bf16[32,2048]{1,0:T(8,128)(2,1)} %param.12) | copy-start | bytes 393220
  115.7 1.6 collective-permute-start.1
  117.6 6.5 %collective-permute-start.3 = (bf16[32,2048]{1,0:T(8,128)(2,1)S(1)}, bf16[32,2048]{1,0:T(8,128)(2,1)S(1)}, u32[]{:S(2)}, u32[]{:S(2)}) collective-permute-start(bf16[32,2048]{1,0:T(8,128)(2,1)S(1)} %get-tuple-element.31), channel_id=1, source_target_pairs={{16,0},{17,1},{18,2},{19,3},{20,4},{21,5},{22,6},{23,7},{24,8},{25... | collective-permute-start | bytes 393224 | tf_op jit(solution)/shard_map/ppermute | solution.py:31
  121.1 7.2 %collective-permute-start.2 = (bf16[32,2048]{1,0:T(8,128)(2,1)S(1)}, bf16[32,2048]{1,0:T(8,128)(2,1)S(1)}, u32[]{:S(2)}, u32[]{:S(2)}) collective-permute-start(bf16[32,2048]{1,0:T(8,128)(2,1)S(1)} %get-tuple-element.30), channel_id=1, source_target_pairs={{0,16},{1,17},{2,18},{3,19},{4,20},{5,21},{6,22},{7,23},{8,24},{9,... | collective-permute-start | bytes 393224 | tf_op jit(solution)/shard_map/ppermute | solution.py:31
  128.2 2.2 %copy-start.1 = (bf16[8,256,1024]{2,1,0:T(8,128)(2,1)S(1)}, bf16[8,256,1024]{2,1,0:T(8,128)(2,1)}, u32[]{:S(2)}) copy-start(bf16[8,256,1024]{2,1,0:T(8,128)(2,1)} %get-tuple-element.28) | copy-start | bytes 12582916
  138.4 2.0 copy-start.5
  138.5 1.9 copy-start.7
  138.5 1.6 collective-permute-start.4

commit v5 on v4

--- a/solution.py
+++ b/solution.py
@@ -113,10 +113,10 @@
 
     def begin(self, chosen):
         for c in chosen:
+            self.pass_on(self.up, c, self.me, self.me + self.wide, True)
+            self.pass_on(self.down, c, self.me, self.me - self.wide, True)
             for peer in self.across:
                 self.pass_on(None, c, self.me, peer, True)
-            self.pass_on(self.up, c, self.me, self.me + self.wide, True)
-            self.pass_on(self.down, c, self.me, self.me - self.wide, True)
 
     def take(self, cond, c, shard):
         arrive = functools.partial(
@@ -167,7 +167,7 @@
     meet([{"dp": j} for j in along + across])
     sends = Sends(send)
     pieces = cut(in_ref, full_in, depth, 4) + cut(out_ref, full_out, depth, 4)
-    relay = Relay(count, pieces, (0,), sends, recv)
+    relay = Relay(count, pieces, (), sends, recv)
     order = list(range(8))
     relay.begin(order)
     mine = [
@@ -238,7 +238,7 @@
 
 def gather_weights(w_in, w_out):
     count = lax.axis_size("dp")
-    sent = relayed(count, 8, 1)
+    sent = relayed(count, 8, 0)
     return pl.pallas_call(
         functools.partial(weights_kernel, count),
         out_shape=[jax.ShapeDtypeStruct((count,) + w.shape, w.dtype) for w in (w_in, w_out)],

time: 208 us -> 206 us (level)
  Pallas kernels: 171 us -> 168 us
    pallas_call x1, Pallas kernels: 52.1 us -> 44.1 us  [exchange_grads(): pl.pallas_call(functools.partial(grads_kernel, count), out_shape=[jax.Sha...]
    pallas_call x1, Pallas kernels: 102 us -> 108 us  [gather_weights(): pl.pallas_call(functools.partial(weights_kernel, count), out_shape=[jax.S...]
  transfers between devices with their start and end apart: 5 -> 5, of which waited for: 4 -> 4; matrix products, arithmetic and copies ran while one was open for 1% -> 1% of each run, Pallas kernels for 50% -> 53%
where the time goes in v5:
time: 206 us; the launch traced here: 203 us
  Pallas kernels  168 us (82%)
  waiting for transfers between devices  8.61 us (4%)
  local copies, waits for them, and re-layouts  7.49 us (4%)
  other arithmetic  7.23 us (4%)
  starting transfers between devices  5.62 us (3%)
  matrix products  4.51 us (2%)
    pallas_call x1, Pallas kernels, gather_weights(): pl.pallas_call(functools.partial(weights_kernel, count), out_shape=[jax.S...  108 us
    pallas_call x1, Pallas kernels, exchange_grads(): pl.pallas_call(functools.partial(grads_kernel, count), out_shape=[jax.Sha...  44.1 us
    pallas_call x2, Pallas kernels, run_slot(): pl.pallas_call(slot_kernel, out_shape=[shape((2 * rows, width), jnp.bfloa...  16 us
    ppermute x2, waiting for transfers between devices, passed_along(): return lax.ppermute(array, axis, pairs)  5.65 us
    ppermute x2, starting transfers between devices, passed_along(): return lax.ppermute(array, axis, pairs)  4.9 us
    unnamed x24, local copies, waits for them, and re-layouts  4.45 us
  transfers between devices with their start and end apart: 5, of which 4 were waited for; matrix products, arithmetic and copies ran while one was open for 1% of the time, Pallas kernels for 53%

profile of v5, /device:TPU:12, one launch (start us, length us, event | category | flops | bytes accessed | tf_op | source)
XLA Modules:
  0.0 202.7 jit_solution(10820380994853056543)
XLA Ops:
  0.6 0.6 collective-permute-start
  1.2 2.0 pad_maximum_fusion.in_ref
  3.2 0.1 fusion.4
  3.3 107.6 %shard_map.170 = (bf16[8,256,1280]{2,1,0:T(8,128)(2,1)}, bf16[8,256,1024]{2,1,0:T(8,128)(2,1)}) custom-call(bf16[256,1280]{1,0:T(8,128)(2,1)} %pad_maximum_fusion.in_ref, bf16[256,1024]{1,0:T(8,128)(2,1)} %bitcast.65), custom_call_target="tpu_custom_call" | custom-call | tf_op jit(solution)/shard_map/pallas_call | solution.py:242
  110.9 0.1 maximum_bitcast_fusion.2
  111.0 0.0 collective-permute-done
  111.0 0.1 tile.4
  111.1 0.0 copy-done.2
  111.1 0.0 copy-done.3
  111.1 0.0 copy-done.8
  111.1 0.0 copy-done.9
  111.1 0.0 copy-start
  111.1 2.2 %copy-done = bf16[8,256,1024]{2,1,0:T(8,128)(2,1)S(1)} copy-done((bf16[8,256,1024]{2,1,0:T(8,128)(2,1)S(1)}, bf16[8,256,1024]{2,1,0:T(8,128)(2,1)}, u32[]{:S(2)}) %copy-start) | copy-done | bytes 4194328
  113.3 8.0 %shard_map.171 = (bf16[64,2048]{1,0:T(8,128)(2,1)S(1)}, bf16[32,2304]{1,0:T(8,128)(2,1)S(1)}, bf16[2,32,2048]{2,1,0:T(8,128)(2,1)S(1)}, f32[2,128]{1,0:T(2,128)S(1)}) custom-call(bf16[32,2048]{1,0:T(8,128)(2,1)S(1)} %bitcast.48, bf16[32,2048]{1,0:T(8,128)(2,1)S(1)} %get-tuple-element.51.xb_ref, bf16[32,2048]{1,0:T(8,128)(2,1)S(1)} %bitcast.50, ...), custom_call_target="tpu_custom_call" | custom-call | tf_op jit(solution)/shard_map/pallas_call | solution.py:403
  121.4 0.0 copy-start.4
  121.4 0.0 copy-start.6
  121.4 0.0 copy-start.11
  121.4 0.1 collective-permute-start.1
  121.5 1.5 collective-permute-done.1.other_ref
  123.0 0.3 shard_map.172
  123.3 0.0 copy-done.4
  123.3 0.0 copy-done.6
  123.4 3.4 %collective-permute-start.3 = (bf16[32,2048]{1,0:T(8,128)(2,1)S(1)}, bf16[32,2048]{1,0:T(8,128)(2,1)S(1)}, u32[]{:S(2)}, u32[]{:S(2)}) collective-permute-start(bf16[32,2048]{1,0:T(8,128)(2,1)S(1)} %get-tuple-element.31), channel_id=1, source_target_pairs={{16,0},{17,1},{18,2},{19,3},{20,4},{21,5},{22,6},{23,7},{24,8},{25... | collective-permute-start | bytes 393224 | tf_op jit(solution)/shard_map/ppermute | solution.py:31
  126.8 1.5 collective-permute-start.2
  128.3 1.5 collective-permute-done.3
  129.8 0.0 copy-done.10
  129.8 4.1 %collective-permute-done.2 = bf16[32,2048]{1,0:T(8,128)(2,1)S(1)} collective-permute-done((bf16[32,2048]{1,0:T(8,128)(2,1)S(1)}, bf16[32,2048]{1,0:T(8,128)(2,1)S(1)}, u32[]{:S(2)}, u32[]{:S(2)}) %collective-permute-start.2) | collective-permute-done | bytes 131104 | tf_op jit(solution)/shard_map/ppermute | solution.py:31
  134.0 0.0 copy-done.11
  134.0 0.0 copy-start.1
  134.0 2.2 %copy-done.1 = bf16[8,256,1024]{2,1,0:T(8,128)(2,1)S(1)} copy-done((bf16[8,256,1024]{2,1,0:T(8,128)(2,1)S(1)}, bf16[8,256,1024]{2,1,0:T(8,128)(2,1)}, u32[]{:S(2)}) %copy-start.1) | copy-done | bytes 4194328
  136.2 8.0 %shard_map.173 = (bf16[64,2048]{1,0:T(8,128)(2,1)S(1)}, bf16[32,2304]{1,0:T(8,128)(2,1)S(1)}, bf16[2,32,2048]{2,1,0:T(8,128)(2,1)S(1)}, f32[2,128]{1,0:T(2,128)S(1)}) custom-call(bf16[32,2048]{1,0:T(8,128)(2,1)S(1)} %broadcast_select_fusion.1.xf_ref, bf16[32,2048]{1,0:T(8,128)(2,1)S(1)} %get-tuple-element.50.xb_ref, ...), custom_call_target="tpu_custom_call" | custom-call | tf_op jit(solution)/shard_map/pallas_call | solution.py:403
  144.2 0.0 copy-start.5
  144.2 0.0 copy-start.7
  144.2 0.1 collective-permute-start.4
  144.3 0.1 pad.2.clone
  144.4 1.4 collective-permute-done.4.other_ref
  145.8 0.3 shard_map.174
  146.2 0.7 maximum_multiply_fusion.small_ref
  146.8 44.1 %shard_map.175 = (bf16[8,2,32,2304]{3,2,1,0:T(8,128)(2,1)}, bf16[8,2,2,32,256]{4,3,2,1,0:T(8,128)(2,1)}, f32[2,8,24,128]{3,2,1,0:T(8,128)}) custom-call(bf16[32,2304]{1,0:T(8,128)(2,1)} %copy-done.6, bf16[32,2304]{1,0:T(8,128)(2,1)} %copy-done.7, bf16[2,32,2048]{2,1,0:T(8,128)(2,1)} %copy-done.4, bf16[2,32,2048]{2,1,0:T(8,128)(2,1)} %copy-done.5, ...), custom_call_target="tpu_custom_call" | custom-call | tf_op jit(solution)/shard_map/pallas_call | solution.py:260
  191.0 1.1 fusion.6
  192.1 1.8 convolution_multiply_fusion
  193.9 1.1 slice_bitcast_fusion
  195.0 0.7 slice_bitcast_fusion.1
  195.7 1.4 slice_reduce_fusion
  197.2 1.4 slice_reduce_fusion.1
  198.6 2.7 %fusion = f32[1,256,1024]{2,1,0:T(8,128)} fusion(bf16[512,256]{1,0:T(8,128)(2,1)S(1)} %bitcast.62, bf16[512,2304]{1,0:T(8,128)(2,1)} %bitcast.61), kind=kOutput, calls=%fused_computation.2 | convolution fusion | flops 268697600 | bytes 2359296 | tf_op jit(solution)/shard_map/dot_general | solution.py:495
  201.3 0.7 maximum_bitcast_fusion.1
  202.0 0.7 maximum_bitcast_fusion
  (15 shorter events, 0.1 us)
Async XLA Ops:
  0.6 110.4 %collective-permute-start = (bf16[2,32,2048]{2,1,0:T(8,128)(2,1)}, bf16[2,32,2048]{2,1,0:T(8,128)(2,1)S(1)}, u32[]{:S(2)}, u32[]{:S(2)}) collective-permute-start(bf16[2,32,2048]{2,1,0:T(8,128)(2,1)} %bitcast.72), channel_id=1, source_target_pairs={{0,16},{16,0},{1,17},{17,1},{2,18},{18,2},{3,19},{19,3},{4,20},{20... | collective-permute-start | bytes 786440 | tf_op jit(solution)/shard_map/ppermute | solution.py:25
  3.2 107.9 %copy-start.2 = (bf16[1,32,2048]{2,1,0:T(8,128)(2,1)S(1)}, bf16[1,32,2048]{2,1,0:T(8,128)(2,1)}, u32[]{:S(2)}) copy-start(bf16[1,32,2048]{2,1,0:T(8,128)(2,1)} %param.11) | copy-start | bytes 393220
  3.2 107.9 %copy-start.3 = (bf16[1,32,2048]{2,1,0:T(8,128)(2,1)S(1)}, bf16[1,32,2048]{2,1,0:T(8,128)(2,1)}, u32[]{:S(2)}) copy-start(bf16[1,32,2048]{2,1,0:T(8,128)(2,1)} %param.13) | copy-start | bytes 393220
  3.2 107.9 %copy-start.8 = (f32[1,2048]{1,0:T(1,128)S(1)}, f32[1,2048]{1,0:T(1,128)}, u32[]{:S(2)}) copy-start(f32[1,2048]{1,0:T(1,128)} %gain_ref.7) | copy-start | bytes 24580
  3.2 107.9 %copy-start.9 = (f32[1,2,128]{2,1,0:T(2,128)S(1)}, f32[1,2,128]{2,1,0:T(2,128)}, u32[]{:S(2)}) copy-start(f32[1,2,128]{2,1,0:T(2,128)} %param.17) | copy-start | bytes 3076
  111.1 2.2 %copy-start = (bf16[8,256,1024]{2,1,0:T(8,128)(2,1)S(1)}, bf16[8,256,1024]{2,1,0:T(8,128)(2,1)}, u32[]{:S(2)}) copy-start(bf16[8,256,1024]{2,1,0:T(8,128)(2,1)} %get-tuple-element.28) | copy-start | bytes 12582916
  113.3 16.5 %copy-start.10 = (bf16[32,2048]{1,0:T(8,128)(2,1)S(1)}, bf16[32,2048]{1,0:T(8,128)(2,1)}, u32[]{:S(2)}) copy-start(bf16[32,2048]{1,0:T(8,128)(2,1)} %param.14) | copy-start | bytes 393220
  121.4 2.0 copy-start.4
  121.4 1.9 copy-start.6
  121.4 12.5 %copy-start.11 = (bf16[32,2048]{1,0:T(8,128)(2,1)S(1)}, bf16[32,2048]{1,0:T(8,128)(2,1)}, u32[]{:S(2)}) copy-start(bf16[32,2048]{1,0:T(8,128)(2,1)} %param.12) | copy-start | bytes 393220
  121.4 1.6 collective-permute-start.1
  123.4 6.5 %collective-permute-start.3 = (bf16[32,2048]{1,0:T(8,128)(2,1)S(1)}, bf16[32,2048]{1,0:T(8,128)(2,1)S(1)}, u32[]{:S(2)}, u32[]{:S(2)}) collective-permute-start(bf16[32,2048]{1,0:T(8,128)(2,1)S(1)} %get-tuple-element.31), channel_id=1, source_target_pairs={{16,0},{17,1},{18,2},{19,3},{20,4},{21,5},{22,6},{23,7},{24,8},{25... | collective-permute-start | bytes 393224 | tf_op jit(solution)/shard_map/ppermute | solution.py:31
  126.8 7.2 %collective-permute-start.2 = (bf16[32,2048]{1,0:T(8,128)(2,1)S(1)}, bf16[32,2048]{1,0:T(8,128)(2,1)S(1)}, u32[]{:S(2)}, u32[]{:S(2)}) collective-permute-start(bf16[32,2048]{1,0:T(8,128)(2,1)S(1)} %get-tuple-element.30), channel_id=1, source_target_pairs={{0,16},{1,17},{2,18},{3,19},{4,20},{5,21},{6,22},{7,23},{8,24},{9,... | collective-permute-start | bytes 393224 | tf_op jit(solution)/shard_map/ppermute | solution.py:31
  134.0 2.2 %copy-start.1 = (bf16[8,256,1024]{2,1,0:T(8,128)(2,1)S(1)}, bf16[8,256,1024]{2,1,0:T(8,128)(2,1)}, u32[]{:S(2)}) copy-start(bf16[8,256,1024]{2,1,0:T(8,128)(2,1)} %get-tuple-element.28) | copy-start | bytes 12582916
  144.2 2.0 copy-start.5
  144.2 1.9 copy-start.7
  144.2 1.6 collective-permute-start.4
